TPU v7x, 256 devices: a whole 4x4x8 slice. The times are simulated.
256 devices in a mesh: prow: 8 (over y, core), pcol: 32 (over x, z).
Axes of the slice: x: 4, y: 4, z: 8, core: 2. Of those that a mesh axis runs over, the one named last changes fastest.
Arguments:
- matrix_slab: float32 [2048, 4096], P('pcol', 'prow'), may hold values from -1024 to 1024
- contributions: float32 [8, 1024, 64, 256], P('prow', 'pcol'), may hold values from -3 to 3
- target_column: int32 [8, 1024], P('prow', 'pcol'), may hold values from 0 to 31, as said below
- target_rows: int32 [8, 1024], P('prow', 'pcol'), may hold values from 0 to 1
- live_rows: int32 [8, 1024], P('prow', 'pcol'), may hold values from 1 to 256
- pivot_index: int32 [1, 256], replicated, may hold values from 256 to 4095, as said below
Outputs:
- factored: float32 [2048, 4096], P('pcol', 'prow')
Inputs may be any that keep to these rules, and one draw needn't show every extreme that they name: `pivot_index`: row k lists 256 distinct rows, each (k + 1) * 256 or more. `target_column`: of the 32 blocks held by one device, at most 2 have target column blocks within the columns of one index of pcol, and exactly 2 for some index.
All inputs are finite; a program needn't handle non-finite values.
Results may differ from a plain program's by a relative error of at most 0.0001.
Values sent between devices are 32-bit elements; how exact they have to be, the bound alone decides.
No kernel may reach another device: no remote copies, remote signals or barrier semaphores. Data moves between devices by JAX's collectives and lax.ppermute only.
A program may use at most 128 MiB of HBM per device.

v0:
```python
import functools

import jax
import jax.numpy as jnp
from jax import lax
from jax.experimental import pallas as pl
from jax.experimental.pallas import tpu as pltpu
from jax.sharding import Mesh
from jax.sharding import PartitionSpec as P

SLAB = 2048
PW = 256
NB = 64
TR = 256
CB_DEV = 32
NX = 4
NZ = 8
PROW = 8
OWNERS = PW // NB
ROWS_DEV = 512
G = 8
AX, AZ, AY = "pcol_0", "pcol_1", "prow"
PCOL = (AX, AZ)
HIGHEST = lax.Precision.HIGHEST
F32 = jnp.float32
MIB = 1024 * 1024
VMEM = pl.BlockSpec(memory_space=pltpu.VMEM)
SMEM = pl.BlockSpec(memory_space=pltpu.SMEM)
HBM = pl.BlockSpec(memory_space=pltpu.HBM)


def dotf(a, b):
    return jnp.dot(a, b, precision=HIGHEST, preferred_element_type=F32)


def dot_nt(a, b):
    dims = (((1,), (1,)), ((), ()))
    return lax.dot_general(a, b, dims, precision=HIGHEST, preferred_element_type=F32)


CH = 8


def scatter_kernel(tc_ref, tr_ref, lr_ref, blocks_ref, slab_ref, pan_out, dense_out, *scratch):
    tc, tr, lr, own, buf, dense, pan, in_sem, num_sem, out_sem = scratch
    my_x = lax.axis_index(AX)
    my_z = lax.axis_index(AZ)
    owner = (my_x == 0) & (my_z < OWNERS)
    numbers = [
        pltpu.make_async_copy(src, dst, num_sem.at[i])
        for i, (src, dst) in enumerate(((tc_ref, tc), (tr_ref, tr), (lr_ref, lr), (slab_ref, own)))
    ]
    for number in numbers:
        number.start()
    loads = [
        pltpu.make_async_copy(blocks_ref.at[pl.ds(i * CH, CH)], buf.at[pl.ds(i * CH, CH)], in_sem.at[i])
        for i in range(CB_DEV // CH)
    ]
    for load in loads:
        load.start()

    def clear(i, carry):
        dense[i] = jnp.zeros((NB, ROWS_DEV), F32)
        return carry

    lax.fori_loop(0, NX * NZ, clear, 0)
    for number in numbers:
        number.wait()
    for i in range(OWNERS):
        pan[i] = jnp.where(owner & (my_z == i), own[...], 0.0)
    lane = lax.broadcasted_iota(jnp.int32, (NB, TR), 1)

    def add(i, carry):
        col = tc[0, i]
        at = pl.ds(pl.multiple_of(tr[0, i] * TR, TR), TR)
        block = jnp.where(lane < lr[0, i], buf[i], 0.0)

        @pl.when(col < OWNERS)
        def _():
            pan[col, :, at] = pan[col, :, at] + block

        @pl.when(col >= OWNERS)
        def _():
            slot = (col % NZ) * NX + (col // NZ + NX - my_x) % NX
            dense[slot, :, at] = dense[slot, :, at] + block

        return carry

    for i in range(CB_DEV // CH):
        loads[i].wait()
        lax.fori_loop(i * CH, (i + 1) * CH, add, 0)
    stores = [
        pltpu.make_async_copy(pan, pan_out, out_sem.at[0]),
        pltpu.make_async_copy(dense, dense_out, out_sem.at[1]),
    ]
    for store in stores:
        store.start()
    for store in stores:
        store.wait()


def scatter(tc, tr, lr, blocks, slab):
    return pl.pallas_call(
        scatter_kernel,
        out_shape=[
            jax.ShapeDtypeStruct((OWNERS, NB, ROWS_DEV), F32),
            jax.ShapeDtypeStruct((NX * NZ, NB, ROWS_DEV), F32),
        ],
        in_specs=[HBM] * 5,
        out_specs=[HBM] * 2,
        scratch_shapes=[pltpu.SMEM((1, CB_DEV), jnp.int32)] * 3
        + [
            pltpu.VMEM((NB, ROWS_DEV), F32),
            pltpu.VMEM((CB_DEV, NB, TR), F32),
            pltpu.VMEM((NX * NZ, NB, ROWS_DEV), F32),
            pltpu.VMEM((OWNERS, NB, ROWS_DEV), F32),
            pltpu.SemaphoreType.DMA((CB_DEV // CH,)),
            pltpu.SemaphoreType.DMA((4,)),
            pltpu.SemaphoreType.DMA((2,)),
        ],
        compiler_params=pltpu.CompilerParams(vmem_limit_bytes=56 * MIB),
        name="scatter",
    )(tc, tr, lr, blocks, slab)


def shift(value, axis, n, step):
    return lax.ppermute(value, axis, [(i, (i + step) % n) for i in range(n)])


def ring_sum(rel, halves, axis, n):
    h = halves[0].shape[0]
    ahead = shift(halves[0], axis, n, 1)
    back = shift(halves[1], axis, n, -1)
    for d in range(n // 2 - 1, 0, -1):
        up, down = rel[d], rel[n - d]
        if ahead.shape[0] == h and d == n // 2 - 1:
            up = jnp.concatenate([up[:h] + ahead, up[h:]], axis=0)
            down = jnp.concatenate([down[:h], down[h:] + back], axis=0)
        else:
            up, down = up + ahead, down + back
        ahead = shift(up, axis, n, 1)
        back = shift(down, axis, n, -1)
    return rel[0] + ahead + back


def sum_along_z(dense):
    return lax.psum_scatter(dense.reshape(NZ, NX, NB, ROWS_DEV), AZ, scatter_dimension=0, tiled=True)[0]


def sum_along_x(part):
    rows = [part[i] for i in range(NX)]
    half = rows[NX // 2]
    return ring_sum(rows, (half[: NB // 2], half[NB // 2 :]), AX, NX)


def exchange(value, axis):
    return lax.all_to_all(value, axis, split_axis=0, concat_axis=0, tiled=True)


def gather(value, axis, n):
    copies = jnp.broadcast_to(value, (n, *value.shape))
    return exchange(copies, axis)


def factor_kernel(t_ref, packed_ref, loinv_ref, upinv_ref, x_ref, v_ref, r_ref, lo_ref, ti_ref, b_ref):
    x_ref[...] = t_ref[...]
    b_ref[...] = jnp.zeros_like(b_ref)
    ti_ref[...] = jnp.zeros_like(ti_ref)
    lo_ref[...] = jnp.zeros_like(lo_ref)
    r_ref[...] = jnp.zeros_like(r_ref)
    lane = lax.broadcasted_iota(jnp.int32, (G, PW), 1)
    row8 = lax.broadcasted_iota(jnp.int32, (G, 128), 0)
    row = lax.broadcasted_iota(jnp.int32, (G, PW), 0)
    lane1 = lax.broadcasted_iota(jnp.int32, (1, PW), 1)
    panel = t_ref[0:G, :]
    steps = PW // G
    for b in range(steps):
        k0 = G * b
        inblk = (lane >= k0) & (lane < k0 + G)
        cols = [jnp.broadcast_to(panel[:, k0 + j : k0 + j + 1], (G, 128)) for j in range(G)]
        nxt = None
        if b + 1 < steps:
            below = x_ref[k0 + G : k0 + 2 * G, :]
            mult = [jnp.broadcast_to(below[:, k0 + j : k0 + j + 1], (G, PW)) for j in range(G)]
            nxt = jnp.where(inblk, 0.0, below)
        lo_block = jnp.zeros((G, PW), F32)
        for k in range(G):
            ck = cols[k]
            inv = 1.0 / jnp.broadcast_to(ck[k : k + 1, :], (G, 128))
            inv2 = jnp.concatenate([inv, inv], axis=1)
            ck2 = jnp.concatenate([ck, ck], axis=1)
            for j in range(k + 1, G):
                m = jnp.broadcast_to(cols[j][k : k + 1, :], (G, 128)) * inv
                cols[j] = jnp.where(row8 == k, m, cols[j] - ck * m)
            lo_block = jnp.where((lane == k0 + k) & (row >= k), ck2, lo_block)
            panel = jnp.where(lane == k0 + k, jnp.where(row == k, 1.0, 0.0), panel)
            scaled = jnp.broadcast_to(panel[k : k + 1, :], (G, PW)) * inv2
            v_ref[k0 + k : k0 + k + 1, :] = scaled[0:1]
            panel = jnp.where(row == k, scaled, panel - ck2 * scaled)
        lo_ref[k0 : k0 + G, :] = lo_block
        ti_ref[k0 : k0 + G, :] = jnp.where(inblk, panel, 0.0)
        if nxt is not None:
            for j in range(G):
                nxt = nxt - mult[j] * jnp.broadcast_to(panel[j : j + 1, :], (G, PW))
        tile = (k0 // 128) * 128
        kk = k0 % 128
        slot = b % 2
        if b >= 2:
            old = (k0 - 2 * G) % 128
            b_ref[slot, old : old + G, :] = jnp.zeros((G, PW), F32)
        b_ref[slot, kk : kk + G, :] = panel
        inb = (lane1 >= k0) & (lane1 < k0 + G)
        raw = x_ref[:, tile : tile + 128]
        r_ref[:, tile : tile + 128] = jnp.where(inb[:, tile : tile + 128], raw, r_ref[:, tile : tile + 128])
        if b + 1 < steps:
            x_ref[...] = jnp.where(inb, 0.0, x_ref[...]) - dotf(raw, b_ref[slot])
            x_ref[k0 : k0 + G, :] = -panel
        unit = jnp.where(row == lane - k0, 1.0, 0.0)
        r_ref[k0 : k0 + G, :] = jnp.where(inblk, unit, r_ref[k0 : k0 + G, :])
        panel = nxt
    z = dotf(r_ref[...], dotf(ti_ref[...], lo_ref[...]))
    v = v_ref[...]
    rr = lax.broadcasted_iota(jnp.int32, (PW, PW), 0)
    cc = lax.broadcasted_iota(jnp.int32, (PW, PW), 1)
    same = (rr // G) == (cc // G)
    packed_ref[...] = jnp.where(rr < cc, v, jnp.where(same, lo_ref[...], z))
    loinv_ref[...] = jnp.where(rr >= cc, v, 0.0)
    upinv_ref[...] = jnp.where(rr < cc, z, jnp.where(rr == cc, 1.0, 0.0))


def factor(t):
    return pl.pallas_call(
        factor_kernel,
        out_shape=[jax.ShapeDtypeStruct((PW, PW), F32)] * 3,
        in_specs=[VMEM],
        out_specs=[VMEM] * 3,
        scratch_shapes=[pltpu.VMEM((PW, PW), F32)] * 5 + [pltpu.VMEM((2, 128, PW), F32)],
        compiler_params=pltpu.CompilerParams(vmem_limit_bytes=16 * MIB),
        cost_estimate=pl.CostEstimate(flops=40_000_000, bytes_accessed=60_000_000, transcendentals=0),
        name="factor",
    )(t)


def finish_kernel(pivot_ref, matrix_ref, offers_ref, panel_ref, packed_ref, loinv_ref, upinv_ref, out_ref, low_ref):
    row_group = lax.axis_index(AY)
    col_group = lax.axis_index(AX) * NZ + lax.axis_index(AZ)
    rows = lax.broadcasted_iota(jnp.int32, (PW, ROWS_DEV), 1) + row_group * ROWS_DEV
    pick = jnp.where(pivot_ref[...] == rows, 1.0, 0.0)
    hit = jnp.sum(pick, axis=0, keepdims=True) > 0.0
    low_ref[...] = dotf(loinv_ref[...], panel_ref[...])
    matrix = jnp.where(hit, dotf(offers_ref[0, :, PW:], pick), matrix_ref[...])
    inc = offers_ref[0, :, :PW]
    for i in range(1, PROW):
        inc = inc + offers_ref[i, :, :PW]
    upper = dotf(inc, upinv_ref[...])
    out_ref[...] = matrix - dotf(upper, low_ref[...])

    @pl.when(row_group == 0)
    def _():
        out_ref[:, :PW] = upper

    @pl.when(col_group < OWNERS)
    def _():
        at = pl.ds(pl.multiple_of(col_group * NB, NB), NB)
        out_ref[...] = low_ref[at, :]

        @pl.when(row_group == 0)
        def _():
            out_ref[:, :PW] = packed_ref[at, :]


def finish(pivot, matrix, offers, panel, packed, loinv, upinv):
    return pl.pallas_call(
        finish_kernel,
        out_shape=jax.ShapeDtypeStruct((NB, ROWS_DEV), F32),
        in_specs=[VMEM] * 7,
        out_specs=VMEM,
        scratch_shapes=[pltpu.VMEM((PW, ROWS_DEV), F32)],
        compiler_params=pltpu.CompilerParams(vmem_limit_bytes=16 * MIB),
        name="finish",
    )(pivot, matrix, offers, panel, packed, loinv, upinv)


def per_device(matrix_slab, contributions, target_column, target_rows, live_rows, pivot_index):
    row_group = lax.axis_index(AY)
    pan, dense = scatter(target_column, target_rows, live_rows, contributions[0], matrix_slab)
    pivot = pivot_index[0]
    pick = (pivot[:, None] == row_group * ROWS_DEV + jnp.arange(ROWS_DEV)[None, :]).astype(F32)
    hit = jnp.sum(pick, axis=0) > 0

    with jax.named_scope("panel_sum"):
        chunk = exchange(pan, AX).sum(axis=0)
        chunk = exchange(chunk.reshape(NZ, NB // NZ, ROWS_DEV), AZ).sum(axis=0)
    with jax.named_scope("panel_swap"):
        offer = jnp.concatenate([dot_nt(chunk, pick), chunk[:, :PW]], axis=1)
        offers = gather(offer, AY, PROW)
        diag = offers[:, :, :PW].sum(axis=0)
        moved = offers[0, :, PW:]
        chunk = jnp.where(hit[None, :], dotf(moved, pick), chunk)
    with jax.named_scope("slab_sum"):
        part = sum_along_z(dense)
    with jax.named_scope("panel_gather"):
        both = jnp.concatenate([diag, chunk], axis=1)
        both = gather(both, AZ, NZ).reshape(NB, PW + ROWS_DEV)
        both = gather(both, AX, NX).reshape(PW, PW + ROWS_DEV)
        both, part = lax.optimization_barrier((both, part))
    with jax.named_scope("slab_sum"):
        matrix = matrix_slab + sum_along_x(part)
    with jax.named_scope("slab_swap"):
        offer = jnp.concatenate([dot_nt(matrix, pick), matrix[:, :PW]], axis=1)
        diag = lax.optimization_barrier((both[:, :PW], offer))[0]
        offers = gather(offer, AY, PROW)
    packed, loinv, upinv = factor(diag)
    return finish(pivot[:, None], matrix, offers, both[:, PW:], packed, loinv, upinv)


def solution(mesh):
    torus = Mesh(mesh.devices.reshape(mesh.shape["prow"], NX, NZ), (AY, AX, AZ))
    placed = (
        P(PCOL, AY),
        P(AY, PCOL, None, None),
        P(AY, PCOL),
        P(AY, PCOL),
        P(AY, PCOL),
        P(),
    )
    return jax.shard_map(
        per_device, mesh=torus, in_specs=placed, out_specs=P(PCOL, AY), check_vma=False
    )
```

profile of v0, /device:TPU:1, one launch (start us, length us, event | category | flops | bytes accessed | tf_op | source)
XLA Modules:
  0.0 136.3 jit_solution(3027888678987737157)
XLA Ops:
  6.5 4.7 %scatter.1 = (f32[4,64,512]{2,1,0:T(8,128)}, f32[32,64,512]{2,1,0:T(8,128)}) custom-call(s32[1,32]{1,0:T(1,128)} %tc_ref.1, s32[1,32]{1,0:T(1,128)} %tr_ref.1, s32[1,32]{1,0:T(1,128)} %lr_ref.1, f32[32,64,256]{2,1,0:T(8,128)} %bitcast.34, f32[64,512]{1,0:T(8,128)} %slab_ref.1), custom_call_target="tpu_custom_call" | custom-call | tf_op jit(solution)/shard_map/scatter/pallas_call | solution.py:103
  11.3 5.0 %all-to-all-start = ((f32[4,64,512]{2,1,0:T(8,128)}), f32[4,64,512]{2,1,0:T(8,128)S(1)}, u32[]{:S(2)}, u32[]{:S(2)}) async-start(f32[4,64,512]{2,1,0:T(8,128)} %get-tuple-element.13), calls=%async_computation | async-start | bytes 1048576 | tf_op jit(solution)/shard_map/panel_sum/all_to_all | solution.py:157
  16.3 7.4 %all-to-all-done = f32[4,64,512]{2,1,0:T(8,128)S(1)} async-done(((f32[4,64,512]{2,1,0:T(8,128)}), f32[4,64,512]{2,1,0:T(8,128)S(1)}, u32[]{:S(2)}, u32[]{:S(2)}) %all-to-all-start) | async-done | bytes 524320 | tf_op jit(solution)/shard_map/panel_sum/all_to_all | solution.py:157
  23.6 0.7 reduce_sum.36
  24.3 9.1 %all-to-all-start.1 = ((f32[8,8,512]{2,1,0:T(8,128)}), f32[8,8,512]{2,1,0:T(8,128)S(1)}, u32[]{:S(2)}, u32[]{:S(2)}) async-start(f32[8,8,512]{2,1,0:T(8,128)} %bitcast.2), calls=%async_computation.1 | async-start | bytes 262144 | tf_op jit(solution)/shard_map/panel_sum/all_to_all | solution.py:157
  33.4 0.1 fusion.5
  33.5 9.4 %all-to-all-done.1 = f32[8,8,512]{2,1,0:T(8,128)S(1)} async-done(((f32[8,8,512]{2,1,0:T(8,128)}), f32[8,8,512]{2,1,0:T(8,128)S(1)}, u32[]{:S(2)}, u32[]{:S(2)}) %all-to-all-start.1) | async-done | bytes 131104 | tf_op jit(solution)/shard_map/panel_sum/all_to_all | solution.py:157
  42.9 0.4 fusion.3
  43.3 0.7 broadcast_in_dim.22
  44.0 8.1 %all-to-all-start.2 = ((f32[8,8,512]{2,1,0:T(8,128)}), f32[8,8,512]{2,1,0:T(8,128)S(1)}, u32[]{:S(2)}, u32[]{:S(2)}) async-start(f32[8,8,512]{2,1,0:T(8,128)} %broadcast_in_dim.22), calls=%async_computation.2 | async-start | bytes 262144 | tf_op jit(solution)/shard_map/panel_swap/all_to_all | solution.py:157
  52.1 5.3 %all-to-all-done.2 = f32[8,8,512]{2,1,0:T(8,128)S(1)} async-done(((f32[8,8,512]{2,1,0:T(8,128)}), f32[8,8,512]{2,1,0:T(8,128)S(1)}, u32[]{:S(2)}, u32[]{:S(2)}) %all-to-all-start.2) | async-done | bytes 131104 | tf_op jit(solution)/shard_map/panel_swap/all_to_all | solution.py:157
  57.4 0.3 convolution_select_fusion
  57.8 15.2 %all_to_all.30 = f32[8,8,768]{2,1,0:T(8,128)S(1)} all-to-all(f32[8,8,768]{2,1,0:T(8,128)S(1)} %broadcast_in_dim.24), channel_id=1, replica_groups=mesh['prow'=8,'pcol_0'=4,'pcol_1'=8] {'pcol_1'}, dimensions={0} | all-to-all | bytes 393216 | tf_op jit(solution)/shard_map/panel_gather/all_to_all | solution.py:157
  73.0 0.1 broadcast_in_dim.25
  73.0 13.1 %all_to_all.31 = f32[4,64,768]{2,1,0:T(8,128)S(1)} all-to-all(f32[4,64,768]{2,1,0:T(8,128)S(1)} %broadcast_in_dim.25), channel_id=1, replica_groups=mesh['prow'=8,'pcol_0'=4,'pcol_1'=8] {'pcol_0'}, dimensions={0} | all-to-all | bytes 1572864 | tf_op jit(solution)/shard_map/panel_gather/all_to_all | solution.py:157
  86.1 1.0 slice_bitcast_fusion.3
  87.1 0.4 collective-permute-start
  87.4 2.4 %collective-permute-start.2 = (f32[32,512]{1,0:T(8,128)S(1)}, f32[32,512]{1,0:T(8,128)S(1)}, u32[]{:S(2)}, u32[]{:S(2)}) collective-permute-start(f32[32,512]{1,0:T(8,128)S(1)} %get-tuple-element.24), channel_id=1, source_target_pairs={{0,24},{8,0},{16,8},{24,16},{1,25},{9,1},{17,9},{25,17},{2,26},{10... | collective-permute-start | bytes 196616 | tf_op jit(solution)/shard_map/slab_sum/ppermute | solution.py:127
  89.8 1.6 %collective-permute-done = f32[32,512]{1,0:T(8,128)S(1)} collective-permute-done((f32[32,512]{1,0:T(8,128)S(1)}, f32[32,512]{1,0:T(8,128)S(1)}, u32[]{:S(2)}, u32[]{:S(2)}) %collective-permute-start) | collective-permute-done | bytes 65568 | tf_op jit(solution)/shard_map/slab_sum/ppermute | solution.py:127
  91.5 0.9 bitcast_add_fusion.2
  92.4 2.8 %collective-permute-start.3 = (f32[64,512]{1,0:T(8,128)S(1)}, f32[64,512]{1,0:T(8,128)S(1)}, u32[]{:S(2)}, u32[]{:S(2)}) collective-permute-start(f32[64,512]{1,0:T(8,128)S(1)} %pad_maximum_fusion.1), channel_id=1, source_target_pairs={{0,24},{8,0},{16,8},{24,16},{1,25},{9,1},{17,9},{25,17},{2,26},{10... | collective-permute-start | bytes 393224 | tf_op jit(solution)/shard_map/slab_sum/ppermute | solution.py:127
  95.2 0.1 collective-permute-start.1
  95.3 1.8 %collective-permute-done.3 = f32[64,512]{1,0:T(8,128)S(1)} collective-permute-done((f32[64,512]{1,0:T(8,128)S(1)}, f32[64,512]{1,0:T(8,128)S(1)}, u32[]{:S(2)}, u32[]{:S(2)}) %collective-permute-start.3) | collective-permute-done | bytes 131104 | tf_op jit(solution)/shard_map/slab_sum/ppermute | solution.py:127
  97.1 3.2 %collective-permute-done.1 = f32[64,512]{1,0:T(8,128)S(1)} collective-permute-done((f32[64,512]{1,0:T(8,128)S(1)}, f32[64,512]{1,0:T(8,128)S(1)}, u32[]{:S(2)}, u32[]{:S(2)}) %collective-permute-start.1) | collective-permute-done | bytes 131104 | tf_op jit(solution)/shard_map/slab_sum/ppermute | solution.py:127
  100.3 0.9 fusion.13.matrix_ref
  101.2 0.4 fusion
  101.7 1.1 broadcast_in_dim.26
  102.8 8.9 %all-to-all-start.5 = ((f32[8,64,512]{2,1,0:T(8,128)}), f32[8,64,512]{2,1,0:T(8,128)S(1)}, u32[]{:S(2)}, u32[]{:S(2)}) async-start(f32[8,64,512]{2,1,0:T(8,128)} %broadcast_in_dim.26), calls=%async_computation.6 | async-start | bytes 2097152 | tf_op jit(solution)/shard_map/slab_swap/all_to_all | solution.py:157
  111.7 0.1 copy.8.pivot_ref
  111.9 0.1 slice.83.panel_ref
  111.9 15.4 %factor.1 = (f32[256,256]{1,0:T(8,128)S(1)}, f32[256,256]{1,0:T(8,128)S(1)}, f32[256,256]{1,0:T(8,128)S(1)}) custom-call(f32[256,256]{1,0:T(8,128)S(1)} %slice.84.t_ref), custom_call_target="tpu_custom_call" | custom-call | flops 40000000 | bytes 60000000 | tf_op jit(solution)/shard_map/factor/pallas_call | solution.py:232
  127.4 2.1 %finish.1 = f32[64,512]{1,0:T(8,128)} custom-call(s32[256,1]{1,0:T(8,128)S(1)} %copy.8.pivot_ref, f32[64,512]{1,0:T(8,128)S(1)} %fusion.13.matrix_ref, f32[8,64,512]{2,1,0:T(8,128)S(1)} %all-to-all-done.5.offers_ref, f32[256,512]{1,0:T(8,128)S(1)} %slice.83.panel_ref, f32[256,256]{1,0:T(8,128)S(1)} %get-tuple-element.18.packed_ref, ...), custom_call_target="tpu_custom_call" | custom-call | tf_op jit(solution)/shard_map/finish/pallas_call | solution.py:273
  (22 shorter events, 0.2 us)
Async XLA Ops:
  6.5 79.6 %reduce-scatter.2.cloned.1.call-start = ((), (), s32[]{:S(2)}) async-start(), calls=%async_computation.7 | async-start | bytes 4718592 | tf_op jit(solution)/shard_map/slab_sum/reduce_scatter | solution.py:147
  6.5 26.9 %copy-start.1 = (s32[1,256]{1,0:T(1,128)S(1)}, s32[1,256]{1,0:T(1,128)}, u32[]{:S(2)}) copy-start(s32[1,256]{1,0:T(1,128)} %param.11) | copy-start | bytes 3076
  11.3 89.0 %copy-start = (f32[64,512]{1,0:T(8,128)S(1)}, f32[64,512]{1,0:T(8,128)}, u32[]{:S(2)}) copy-start(f32[64,512]{1,0:T(8,128)} %slab_ref.1) | copy-start | bytes 393220
  11.3 12.3 %all-to-all-start = ((f32[4,64,512]{2,1,0:T(8,128)}), f32[4,64,512]{2,1,0:T(8,128)S(1)}, u32[]{:S(2)}, u32[]{:S(2)}) async-start(f32[4,64,512]{2,1,0:T(8,128)} %get-tuple-element.13), calls=%async_computation | async-start | bytes 1048576 | tf_op jit(solution)/shard_map/panel_sum/all_to_all | solution.py:157
  24.3 18.6 %all-to-all-start.1 = ((f32[8,8,512]{2,1,0:T(8,128)}), f32[8,8,512]{2,1,0:T(8,128)S(1)}, u32[]{:S(2)}, u32[]{:S(2)}) async-start(f32[8,8,512]{2,1,0:T(8,128)} %bitcast.2), calls=%async_computation.1 | async-start | bytes 262144 | tf_op jit(solution)/shard_map/panel_sum/all_to_all | solution.py:157
  44.0 13.4 %all-to-all-start.2 = ((f32[8,8,512]{2,1,0:T(8,128)}), f32[8,8,512]{2,1,0:T(8,128)S(1)}, u32[]{:S(2)}, u32[]{:S(2)}) async-start(f32[8,8,512]{2,1,0:T(8,128)} %broadcast_in_dim.22), calls=%async_computation.2 | async-start | bytes 262144 | tf_op jit(solution)/shard_map/panel_swap/all_to_all | solution.py:157
  87.1 4.4 %collective-permute-start = (f32[32,512]{1,0:T(8,128)S(1)}, f32[32,512]{1,0:T(8,128)S(1)}, u32[]{:S(2)}, u32[]{:S(2)}) collective-permute-start(f32[32,512]{1,0:T(8,128)S(1)} %get-tuple-element.23), channel_id=1, source_target_pairs={{0,8},{8,16},{16,24},{24,0},{1,9},{9,17},{17,25},{25,1},{2,10},{10... | collective-permute-start | bytes 196616 | tf_op jit(solution)/shard_map/slab_sum/ppermute | solution.py:127
  87.4 4.0 %collective-permute-start.2 = (f32[32,512]{1,0:T(8,128)S(1)}, f32[32,512]{1,0:T(8,128)S(1)}, u32[]{:S(2)}, u32[]{:S(2)}) collective-permute-start(f32[32,512]{1,0:T(8,128)S(1)} %get-tuple-element.24), channel_id=1, source_target_pairs={{0,24},{8,0},{16,8},{24,16},{1,25},{9,1},{17,9},{25,17},{2,26},{10... | collective-permute-start | bytes 196616 | tf_op jit(solution)/shard_map/slab_sum/ppermute | solution.py:127
  92.4 4.7 %collective-permute-start.3 = (f32[64,512]{1,0:T(8,128)S(1)}, f32[64,512]{1,0:T(8,128)S(1)}, u32[]{:S(2)}, u32[]{:S(2)}) collective-permute-start(f32[64,512]{1,0:T(8,128)S(1)} %pad_maximum_fusion.1), channel_id=1, source_target_pairs={{0,24},{8,0},{16,8},{24,16},{1,25},{9,1},{17,9},{25,17},{2,26},{10... | collective-permute-start | bytes 393224 | tf_op jit(solution)/shard_map/slab_sum/ppermute | solution.py:127
  95.2 5.1 %collective-permute-start.1 = (f32[64,512]{1,0:T(8,128)S(1)}, f32[64,512]{1,0:T(8,128)S(1)}, u32[]{:S(2)}, u32[]{:S(2)}) collective-permute-start(f32[64,512]{1,0:T(8,128)S(1)} %pad_maximum_fusion), channel_id=1, source_target_pairs={{0,8},{8,16},{16,24},{24,0},{1,9},{9,17},{17,25},{25,1},{2,10},{10... | collective-permute-start | bytes 393224 | tf_op jit(solution)/shard_map/slab_sum/ppermute | solution.py:127
  102.8 24.5 %all-to-all-start.5 = ((f32[8,64,512]{2,1,0:T(8,128)}), f32[8,64,512]{2,1,0:T(8,128)S(1)}, u32[]{:S(2)}, u32[]{:S(2)}) async-start(f32[8,64,512]{2,1,0:T(8,128)} %broadcast_in_dim.26), calls=%async_computation.6 | async-start | bytes 2097152 | tf_op jit(solution)/shard_map/slab_swap/all_to_all | solution.py:157
Sparse Core Ops, SparseCore 0:
  11.4 66.1 reduce-scatter.1
where the time goes:
time: 137 us; the launch traced here: 136 us
  starting transfers between devices  36.6 us (27%)
  waiting for transfers between devices  28.7 us (21%)
  blocking collectives  28.3 us (21%)
  Pallas kernels  22.3 us (16%)
  between operations  13.5 us (10%)
  local copies, waits for them, and re-layouts  3.05 us (2%)
  other arithmetic  2.74 us (2%)
    all_to_all x4, starting transfers between devices, exchange(): return lax.all_to_all(value, axis, split_axis=0, concat_axis=0, tiled=True)  31 us
    all_to_all x2, blocking collectives, exchange(): return lax.all_to_all(value, axis, split_axis=0, concat_axis=0, tiled=True)  28.3 us
    all_to_all x4, waiting for transfers between devices, exchange(): return lax.all_to_all(value, axis, split_axis=0, concat_axis=0, tiled=True)  22 us
    pallas_call x1, Pallas kernels, factor(): pl.pallas_call(factor_kernel, out_shape=[jax.ShapeDtypeStruct((PW, PW), F...  15.4 us
    ppermute x4, waiting for transfers between devices, shift(): return lax.ppermute(value, axis, [(i, (i + step) % n) for i in range(n)])  6.67 us
    ppermute x4, starting transfers between devices, shift(): return lax.ppermute(value, axis, [(i, (i + step) % n) for i in range(n)])  5.59 us
    pallas_call x1, Pallas kernels, scatter(): pl.pallas_call(scatter_kernel, out_shape=[jax.ShapeDtypeStruct((OWNERS, N...  4.73 us
  transfers between devices with their start and end apart: 9, of which 6 were waited for; matrix products, arithmetic and copies ran while one was open for 2% of the time, Pallas kernels for 11%

commit v1 on v0

--- a/solution.py
+++ b/solution.py
@@ -41,8 +41,9 @@
 CH = 8
 
 
-def scatter_kernel(tc_ref, tr_ref, lr_ref, blocks_ref, slab_ref, pan_out, dense_out, *scratch):
-    tc, tr, lr, own, buf, dense, pan, in_sem, num_sem, out_sem = scratch
+def scatter_kernel(tc_ref, tr_ref, lr_ref, blocks_ref, slab_ref, pan_out, *rest):
+    dense_outs = rest[:9]
+    tc, tr, lr, own, buf, dense, pan, in_sem, num_sem, out_sem = rest[9:]
     my_x = lax.axis_index(AX)
     my_z = lax.axis_index(AZ)
     owner = (my_x == 0) & (my_z < OWNERS)
@@ -81,7 +82,7 @@
 
         @pl.when(col >= OWNERS)
         def _():
-            slot = (col % NZ) * NX + (col // NZ + NX - my_x) % NX
+            slot = ((col % NZ + NZ - my_z) % NZ) * NX + (col // NZ + NX - my_x) % NX
             dense[slot, :, at] = dense[slot, :, at] + block
 
         return carry
@@ -89,10 +90,11 @@
     for i in range(CB_DEV // CH):
         loads[i].wait()
         lax.fori_loop(i * CH, (i + 1) * CH, add, 0)
-    stores = [
-        pltpu.make_async_copy(pan, pan_out, out_sem.at[0]),
-        pltpu.make_async_copy(dense, dense_out, out_sem.at[1]),
-    ]
+    stores = [pltpu.make_async_copy(pan, pan_out, out_sem.at[0])]
+    base = 0
+    for i, out in enumerate(dense_outs):
+        stores.append(pltpu.make_async_copy(dense.at[pl.ds(base, out.shape[0])], out, out_sem.at[1 + i]))
+        base += out.shape[0]
     for store in stores:
         store.start()
     for store in stores:
@@ -100,14 +102,12 @@
 
 
 def scatter(tc, tr, lr, blocks, slab):
-    return pl.pallas_call(
+    sizes = [NX] * 4 + [NX // 2] * 2 + [NX] * 3
+    outs = pl.pallas_call(
         scatter_kernel,
-        out_shape=[
-            jax.ShapeDtypeStruct((OWNERS, NB, ROWS_DEV), F32),
-            jax.ShapeDtypeStruct((NX * NZ, NB, ROWS_DEV), F32),
-        ],
+        out_shape=[jax.ShapeDtypeStruct((n, NB, ROWS_DEV), F32) for n in [OWNERS] + sizes],
         in_specs=[HBM] * 5,
-        out_specs=[HBM] * 2,
+        out_specs=[HBM] * 10,
         scratch_shapes=[pltpu.SMEM((1, CB_DEV), jnp.int32)] * 3
         + [
             pltpu.VMEM((NB, ROWS_DEV), F32),
@@ -116,11 +116,12 @@
             pltpu.VMEM((OWNERS, NB, ROWS_DEV), F32),
             pltpu.SemaphoreType.DMA((CB_DEV // CH,)),
             pltpu.SemaphoreType.DMA((4,)),
-            pltpu.SemaphoreType.DMA((2,)),
+            pltpu.SemaphoreType.DMA((10,)),
         ],
         compiler_params=pltpu.CompilerParams(vmem_limit_bytes=56 * MIB),
         name="scatter",
     )(tc, tr, lr, blocks, slab)
+    return outs[0], list(outs[1:])
 
 
 def shift(value, axis, n, step):
@@ -129,28 +130,21 @@
 
 def ring_sum(rel, halves, axis, n):
     h = halves[0].shape[0]
-    ahead = shift(halves[0], axis, n, 1)
-    back = shift(halves[1], axis, n, -1)
+    pair = yield shift(halves[0], axis, n, 1), shift(halves[1], axis, n, -1)
     for d in range(n // 2 - 1, 0, -1):
         up, down = rel[d], rel[n - d]
-        if ahead.shape[0] == h and d == n // 2 - 1:
-            up = jnp.concatenate([up[:h] + ahead, up[h:]], axis=0)
-            down = jnp.concatenate([down[:h], down[h:] + back], axis=0)
+        if d == n // 2 - 1:
+            up = jnp.concatenate([up[:h] + pair[0], up[h:]], axis=0)
+            down = jnp.concatenate([down[:h], down[h:] + pair[1]], axis=0)
         else:
-            up, down = up + ahead, down + back
-        ahead = shift(up, axis, n, 1)
-        back = shift(down, axis, n, -1)
-    return rel[0] + ahead + back
-
-
-def sum_along_z(dense):
-    return lax.psum_scatter(dense.reshape(NZ, NX, NB, ROWS_DEV), AZ, scatter_dimension=0, tiled=True)[0]
-
-
-def sum_along_x(part):
-    rows = [part[i] for i in range(NX)]
-    half = rows[NX // 2]
-    return ring_sum(rows, (half[: NB // 2], half[NB // 2 :]), AX, NX)
+            up, down = up + pair[0], down + pair[1]
+        pair = yield shift(up, axis, n, 1), shift(down, axis, n, -1)
+    yield rel[0] + pair[0] + pair[1]
+
+
+def tied(value, pair):
+    value, first, second = lax.optimization_barrier((value, *pair))
+    return value, (first, second)
 
 
 def exchange(value, axis):
@@ -288,24 +282,29 @@
     pick = (pivot[:, None] == row_group * ROWS_DEV + jnp.arange(ROWS_DEV)[None, :]).astype(F32)
     hit = jnp.sum(pick, axis=0) > 0
 
-    with jax.named_scope("panel_sum"):
-        chunk = exchange(pan, AX).sum(axis=0)
-        chunk = exchange(chunk.reshape(NZ, NB // NZ, ROWS_DEV), AZ).sum(axis=0)
-    with jax.named_scope("panel_swap"):
-        offer = jnp.concatenate([dot_nt(chunk, pick), chunk[:, :PW]], axis=1)
-        offers = gather(offer, AY, PROW)
-        diag = offers[:, :, :PW].sum(axis=0)
-        moved = offers[0, :, PW:]
-        chunk = jnp.where(hit[None, :], dotf(moved, pick), chunk)
-    with jax.named_scope("slab_sum"):
-        part = sum_along_z(dense)
-    with jax.named_scope("panel_gather"):
-        both = jnp.concatenate([diag, chunk], axis=1)
-        both = gather(both, AZ, NZ).reshape(NB, PW + ROWS_DEV)
-        both = gather(both, AX, NX).reshape(PW, PW + ROWS_DEV)
-        both, part = lax.optimization_barrier((both, part))
-    with jax.named_scope("slab_sum"):
-        matrix = matrix_slab + sum_along_x(part)
+    along_z = ring_sum(dense[:4] + [None] + dense[6:], (dense[4], dense[5]), AZ, NZ)
+    pair = next(along_z)
+    chunk, pair = tied(exchange(pan, AX), pair)
+    pair = along_z.send(pair)
+    chunk = exchange(chunk.sum(axis=0).reshape(NZ, NB // NZ, ROWS_DEV), AZ)
+    chunk, pair = tied(chunk, pair)
+    pair = along_z.send(pair)
+    chunk = chunk.sum(axis=0)
+    offer = jnp.concatenate([dot_nt(chunk, pick), chunk[:, :PW]], axis=1)
+    offers, pair = tied(gather(offer, AY, PROW), pair)
+    pair = along_z.send(pair)
+    moved = offers[0, :, PW:]
+    chunk = jnp.where(hit[None, :], dotf(moved, pick), chunk)
+    both = jnp.concatenate([offers[:, :, :PW].sum(axis=0), chunk], axis=1)
+    both, pair = tied(gather(both, AZ, NZ), pair)
+    part = along_z.send(pair)
+    half = part[NX // 2]
+    along_x = ring_sum([part[0], part[1], None, part[3]], (half[: NB // 2], half[NB // 2 :]), AX, NX)
+    pair = next(along_x)
+    both, pair = tied(gather(both.reshape(NB, PW + ROWS_DEV), AX, NX), pair)
+    both = both.reshape(PW, PW + ROWS_DEV)
+    pair = along_x.send(pair)
+    matrix = matrix_slab + along_x.send(pair)
     with jax.named_scope("slab_swap"):
         offer = jnp.concatenate([dot_nt(matrix, pick), matrix[:, :PW]], axis=1)
         diag = lax.optimization_barrier((both[:, :PW], offer))[0]

time: 137 us -> 127 us (0.927)
  blocking collectives: 28.3 us -> 13.5 us
  starting transfers between devices: 36.6 us -> 50.5 us
  between operations: 13.5 us -> 0.23 us
  other arithmetic: 2.74 us -> 5.25 us
  waiting for transfers between devices: 28.7 us -> 30.5 us
    all_to_all x2 -> x1, blocking collectives: 28.3 us -> 13.5 us  [exchange(): return lax.all_to_all(value, axis, split_axis=0, concat_axis=0, tiled=True)]
    ppermute x4 -> x12, starting transfers between devices: 5.59 us -> 18.3 us  [shift(): return lax.ppermute(value, axis, [(i, (i + step) % n) for i in range(n)])]
    ppermute x4 -> x12, waiting for transfers between devices: 6.67 us -> 16.9 us  [shift(): return lax.ppermute(value, axis, [(i, (i + step) % n) for i in range(n)])]
    all_to_all x4 -> x5, waiting for transfers between devices: 22 us -> 13.6 us  [exchange(): return lax.all_to_all(value, axis, split_axis=0, concat_axis=0, tiled=True)]
    concatenate x3 -> x5, other arithmetic: 0.03 us -> 1.7 us  [the longest x2 0.85 us: ring_sum(): up = jnp.concatenate([up[:h] + pair[0], up[h:]], axis=0)]
    all_to_all x4 -> x5, starting transfers between devices: 31 us -> 32.2 us  [exchange(): return lax.all_to_all(value, axis, split_axis=0, concat_axis=0, tiled=True)]
  transfers between devices with their start and end apart: 9 -> 17, of which waited for: 6 -> 6; matrix products, arithmetic and copies ran while one was open for 2% -> 3% of each run, Pallas kernels for 11% -> 12%
where the time goes in v1:
time: 127 us
  starting transfers between devices  50.5 us (40%)
  waiting for transfers between devices  30.5 us (24%)
  Pallas kernels  22.4 us (18%)
  blocking collectives  13.5 us (11%)
  other arithmetic  5.25 us (4%)
  local copies, waits for them, and re-layouts  3.05 us (2%)
    all_to_all x5, starting transfers between devices, exchange(): return lax.all_to_all(value, axis, split_axis=0, concat_axis=0, tiled=True)  32.2 us
    ppermute x12, starting transfers between devices, shift(): return lax.ppermute(value, axis, [(i, (i + step) % n) for i in range(n)])  18.3 us
    ppermute x12, waiting for transfers between devices, shift(): return lax.ppermute(value, axis, [(i, (i + step) % n) for i in range(n)])  16.9 us
    pallas_call x1, Pallas kernels, factor(): pl.pallas_call(factor_kernel, out_shape=[jax.ShapeDtypeStruct((PW, PW), F...  15.4 us
    all_to_all x5, waiting for transfers between devices, exchange(): return lax.all_to_all(value, axis, split_axis=0, concat_axis=0, tiled=True)  13.6 us
    all_to_all x1, blocking collectives, exchange(): return lax.all_to_all(value, axis, split_axis=0, concat_axis=0, tiled=True)  13.5 us
    pallas_call x1, Pallas kernels, scatter(): pl.pallas_call(scatter_kernel, out_shape=[jax.ShapeDtypeStruct((n, NB, RO...  4.88 us
    broadcast_in_dim x4, local copies, waits for them, and re-layouts, gather(): copies = jnp.broadcast_to(value, (n, *value.shape))  2.78 us
  transfers between devices with their start and end apart: 17, of which 6 were waited for; matrix products, arithmetic and copies ran while one was open for 3% of the time, Pallas kernels for 12%

profile of v1, /device:TPU:1, one launch (start us, length us, event | category | flops | bytes accessed | tf_op | source)
XLA Modules:
  0.0 126.6 jit_solution(9502441682320864890)
XLA Ops:
  0.0 4.9 %scatter.1 = (f32[4,64,512]{2,1,0:T(8,128)}, f32[4,64,512]{2,1,0:T(8,128)}, f32[4,64,512]{2,1,0:T(8,128)}, f32[4,64,512]{2,1,0:T(8,128)}, f32[4,64,512]{2,1,0:T(...) custom-call(s32[1,32]{1,0:T(1,128)} %tc_ref.1, ...), custom_call_target="tpu_custom_call" | custom-call | tf_op jit(solution)/shard_map/scatter/pallas_call | solution.py:106
  4.9 4.9 %all-to-all-start = ((f32[4,64,512]{2,1,0:T(8,128)}), f32[4,64,512]{2,1,0:T(8,128)S(1)}, u32[]{:S(2)}, u32[]{:S(2)}) async-start(f32[4,64,512]{2,1,0:T(8,128)} %get-tuple-element.35), calls=%async_computation | async-start | bytes 1048576 | tf_op jit(solution)/shard_map/all_to_all | solution.py:151
  9.8 1.7 %collective-permute-start = (f32[2,64,512]{2,1,0:T(8,128)}, f32[2,64,512]{2,1,0:T(8,128)S(1)}, u32[]{:S(2)}, u32[]{:S(2)}) collective-permute-start(f32[2,64,512]{2,1,0:T(8,128)} %get-tuple-element.36), channel_id=1, source_target_pairs={{0,1},{1,2},{2,3},{3,4},{4,5},{5,6},{6,7},{7,0},{8,9},{9,10},{10,1... | collective-permute-start | bytes 786440 | tf_op jit(solution)/shard_map/ppermute | solution.py:128
  11.4 3.9 %collective-permute-start.1 = (f32[2,64,512]{2,1,0:T(8,128)}, f32[2,64,512]{2,1,0:T(8,128)S(1)}, u32[]{:S(2)}, u32[]{:S(2)}) collective-permute-start(f32[2,64,512]{2,1,0:T(8,128)} %get-tuple-element.37), channel_id=1, source_target_pairs={{0,7},{1,0},{2,1},{3,2},{4,3},{5,4},{6,5},{7,6},{8,15},{9,8},{10,9... | collective-permute-start | bytes 786440 | tf_op jit(solution)/shard_map/ppermute | solution.py:128
  15.3 5.9 %collective-permute-done = f32[2,64,512]{2,1,0:T(8,128)S(1)} collective-permute-done((f32[2,64,512]{2,1,0:T(8,128)}, f32[2,64,512]{2,1,0:T(8,128)S(1)}, u32[]{:S(2)}, u32[]{:S(2)}) %collective-permute-start) | collective-permute-done | bytes 262176 | tf_op jit(solution)/shard_map/ppermute | solution.py:128
  21.2 1.3 %slice_add_fusion.1 = (f32[2,64,512]{2,1,0:T(8,128)S(1)}, f32[2,64,512]{2,1,0:T(8,128)S(1)}, f32[2,64,512]{2,1,0:T(8,128)S(1)}, f32[2,64,512]{2,1,0:T(8,128)S(1)}) fusion(f32[2,64,512]{2,1,0:T(8,128)S(1)} %collective-permute-done, f32[4,64,512]{2,1,0:T(8,128)} %get-tuple-element.39, f32[2,64,512]{2,1,0:T(8,128)S(1)} %collective-permute-done.1, ...), kind=kLoop, calls=%fused_computation.15 | loop fusion | flops 131072 | bytes 2621440 | tf_op jit(solution)/shard_map/add | solution.py:137
  22.6 0.8 pad_maximum_fusion
  23.4 0.8 pad_maximum_fusion.1
  24.2 2.7 %collective-permute-start.3 = (f32[4,64,512]{2,1,0:T(8,128)}, f32[4,64,512]{2,1,0:T(8,128)S(1)}, u32[]{:S(2)}, u32[]{:S(2)}) collective-permute-start(f32[4,64,512]{2,1,0:T(8,128)} %pad_maximum_fusion.1), channel_id=1, source_target_pairs={{0,7},{1,0},{2,1},{3,2},{4,3},{5,4},{6,5},{7,6},{8,15},{9,8},{10,9... | collective-permute-start | bytes 1572872 | tf_op jit(solution)/shard_map/ppermute | solution.py:128
  26.9 0.7 reduce_sum.36
  27.6 5.1 %all-to-all-start.1 = ((f32[8,8,512]{2,1,0:T(8,128)}), f32[8,8,512]{2,1,0:T(8,128)S(1)}, u32[]{:S(2)}, u32[]{:S(2)}) async-start(f32[8,8,512]{2,1,0:T(8,128)} %bitcast.2), calls=%async_computation.1 | async-start | bytes 262144 | tf_op jit(solution)/shard_map/all_to_all | solution.py:151
  32.9 8.4 %all-to-all-done.1 = f32[8,8,512]{2,1,0:T(8,128)S(1)} async-done(((f32[8,8,512]{2,1,0:T(8,128)}), f32[8,8,512]{2,1,0:T(8,128)S(1)}, u32[]{:S(2)}, u32[]{:S(2)}) %all-to-all-start.1) | async-done | bytes 131104 | tf_op jit(solution)/shard_map/all_to_all | solution.py:151
  41.3 0.9 add.54
  42.2 1.3 %collective-permute-start.4 = (f32[4,64,512]{2,1,0:T(8,128)}, f32[4,64,512]{2,1,0:T(8,128)S(1)}, u32[]{:S(2)}, u32[]{:S(2)}) collective-permute-start(f32[4,64,512]{2,1,0:T(8,128)} %add.54), channel_id=1, source_target_pairs={{0,1},{1,2},{2,3},{3,4},{4,5},{5,6},{6,7},{7,0},{8,9},{9,10},{10,1... | collective-permute-start | bytes 1572872 | tf_op jit(solution)/shard_map/ppermute | solution.py:128
  43.6 1.5 %collective-permute-start.5 = (f32[4,64,512]{2,1,0:T(8,128)S(1)}, f32[4,64,512]{2,1,0:T(8,128)S(1)}, u32[]{:S(2)}, u32[]{:S(2)}) collective-permute-start(f32[4,64,512]{2,1,0:T(8,128)S(1)} %add.55), channel_id=1, source_target_pairs={{0,7},{1,0},{2,1},{3,2},{4,3},{5,4},{6,5},{7,6},{8,15},{9,8},{10,9... | collective-permute-start | bytes 1572872 | tf_op jit(solution)/shard_map/ppermute | solution.py:128
  46.1 8.2 %all-to-all-start.2 = ((f32[8,8,512]{2,1,0:T(8,128)}), f32[8,8,512]{2,1,0:T(8,128)S(1)}, u32[]{:S(2)}, u32[]{:S(2)}) async-start(f32[8,8,512]{2,1,0:T(8,128)} %broadcast_in_dim.22), calls=%async_computation.2 | async-start | bytes 262144 | tf_op jit(solution)/shard_map/all_to_all | solution.py:151
  54.4 5.3 %all-to-all-done.2 = f32[8,8,512]{2,1,0:T(8,128)S(1)} async-done(((f32[8,8,512]{2,1,0:T(8,128)}), f32[8,8,512]{2,1,0:T(8,128)S(1)}, u32[]{:S(2)}, u32[]{:S(2)}) %all-to-all-start.2) | async-done | bytes 131104 | tf_op jit(solution)/shard_map/all_to_all | solution.py:151
  59.7 1.3 collective-permute-start.6
  61.1 1.6 %collective-permute-start.7 = (f32[4,64,512]{2,1,0:T(8,128)S(1)}, f32[4,64,512]{2,1,0:T(8,128)S(1)}, u32[]{:S(2)}, u32[]{:S(2)}) collective-permute-start(f32[4,64,512]{2,1,0:T(8,128)S(1)} %add.57), channel_id=1, source_target_pairs={{0,7},{1,0},{2,1},{3,2},{4,3},{5,4},{6,5},{7,6},{8,15},{9,8},{10,9... | collective-permute-start | bytes 1572872 | tf_op jit(solution)/shard_map/ppermute | solution.py:128
  63.0 13.5 %all_to_all.30 = f32[8,8,768]{2,1,0:T(8,128)S(1)} all-to-all(f32[8,8,768]{2,1,0:T(8,128)S(1)} %broadcast_in_dim.24), channel_id=1, replica_groups=mesh['prow'=8,'pcol_0'=4,'pcol_1'=8] {'pcol_1'}, dimensions={0} | all-to-all | bytes 393216 | tf_op jit(solution)/shard_map/all_to_all | solution.py:151
  76.5 1.0 broadcast_in_dim.25
  77.5 4.0 %all-to-all-start.4 = ((f32[4,64,768]{2,1,0:T(8,128)}), f32[4,64,768]{2,1,0:T(8,128)S(1)}, u32[]{:S(2)}, u32[]{:S(2)}) async-start(f32[4,64,768]{2,1,0:T(8,128)} %broadcast_in_dim.25), calls=%async_computation.4 | async-start | bytes 1572864 | tf_op jit(solution)/shard_map/all_to_all | solution.py:151
  81.7 1.6 %collective-permute-start.8 = (f32[32,512]{1,0:T(8,128)S(1)}, f32[32,512]{1,0:T(8,128)S(1)}, u32[]{:S(2)}, u32[]{:S(2)}) collective-permute-start(f32[32,512]{1,0:T(8,128)S(1)} %get-tuple-element.68), channel_id=1, source_target_pairs={{0,8},{8,16},{16,24},{24,0},{1,9},{9,17},{17,25},{25,1},{2,10},{10... | collective-permute-start | bytes 196616 | tf_op jit(solution)/shard_map/ppermute | solution.py:128
  83.3 1.3 %collective-permute-start.9 = (f32[32,512]{1,0:T(8,128)S(1)}, f32[32,512]{1,0:T(8,128)S(1)}, u32[]{:S(2)}, u32[]{:S(2)}) collective-permute-start(f32[32,512]{1,0:T(8,128)S(1)} %get-tuple-element.67), channel_id=1, source_target_pairs={{0,24},{8,0},{16,8},{24,16},{1,25},{9,1},{17,9},{25,17},{2,26},{10... | collective-permute-start | bytes 196616 | tf_op jit(solution)/shard_map/ppermute | solution.py:128
  84.5 6.2 %collective-permute-done.8 = f32[32,512]{1,0:T(8,128)S(1)} collective-permute-done((f32[32,512]{1,0:T(8,128)S(1)}, f32[32,512]{1,0:T(8,128)S(1)}, u32[]{:S(2)}, u32[]{:S(2)}) %collective-permute-start.8) | collective-permute-done | bytes 65568 | tf_op jit(solution)/shard_map/ppermute | solution.py:128
  90.8 1.3 %collective-permute-start.11 = (f32[64,512]{1,0:T(8,128)S(1)}, f32[64,512]{1,0:T(8,128)S(1)}, u32[]{:S(2)}, u32[]{:S(2)}) collective-permute-start(f32[64,512]{1,0:T(8,128)S(1)} %pad_maximum_fusion.3), channel_id=1, source_target_pairs={{0,24},{8,0},{16,8},{24,16},{1,25},{9,1},{17,9},{25,17},{2,26},{10... | collective-permute-start | bytes 393224 | tf_op jit(solution)/shard_map/ppermute | solution.py:128
  92.5 3.0 %collective-permute-done.11 = f32[64,512]{1,0:T(8,128)S(1)} collective-permute-done((f32[64,512]{1,0:T(8,128)S(1)}, f32[64,512]{1,0:T(8,128)S(1)}, u32[]{:S(2)}, u32[]{:S(2)}) %collective-permute-start.11) | collective-permute-done | bytes 131104 | tf_op jit(solution)/shard_map/ppermute | solution.py:128
  95.5 1.8 %collective-permute-done.10 = f32[64,512]{1,0:T(8,128)S(1)} collective-permute-done((f32[64,512]{1,0:T(8,128)S(1)}, f32[64,512]{1,0:T(8,128)S(1)}, u32[]{:S(2)}, u32[]{:S(2)}) %collective-permute-start.10) | collective-permute-done | bytes 131104 | tf_op jit(solution)/shard_map/ppermute | solution.py:128
  97.8 1.1 broadcast_in_dim.26
  98.9 9.9 %all-to-all-start.5 = ((f32[8,64,512]{2,1,0:T(8,128)}), f32[8,64,512]{2,1,0:T(8,128)S(1)}, u32[]{:S(2)}, u32[]{:S(2)}) async-start(f32[8,64,512]{2,1,0:T(8,128)} %broadcast_in_dim.26), calls=%async_computation.5 | async-start | bytes 2097152 | tf_op jit(solution)/shard_map/slab_swap/all_to_all | solution.py:151
  109.0 15.4 %factor.1 = (f32[256,256]{1,0:T(8,128)S(1)}, f32[256,256]{1,0:T(8,128)S(1)}, f32[256,256]{1,0:T(8,128)S(1)}) custom-call(f32[256,256]{1,0:T(8,128)S(1)} %slice.111.t_ref), custom_call_target="tpu_custom_call" | custom-call | flops 40000000 | bytes 60000000 | tf_op jit(solution)/shard_map/factor/pallas_call | solution.py:226
  124.4 2.1 %finish.1 = f32[64,512]{1,0:T(8,128)} custom-call(s32[256,1]{1,0:T(8,128)S(1)} %copy.8.pivot_ref, f32[64,512]{1,0:T(8,128)S(1)} %fusion.14.matrix_ref, f32[8,64,512]{2,1,0:T(8,128)S(1)} %all-to-all-done.5.offers_ref, f32[256,512]{1,0:T(8,128)S(1)} %slice.110.panel_ref, f32[256,256]{1,0:T(8,128)S(1)} %get-tuple-element.60.packed_ref, ...), custom_call_target="tpu_custom_call" | custom-call | tf_op jit(solution)/shard_map/finish/pallas_call | solution.py:267
  (54 shorter events, 3.2 us)
Async XLA Ops:
  4.9 16.3 %all-to-all-start = ((f32[4,64,512]{2,1,0:T(8,128)}), f32[4,64,512]{2,1,0:T(8,128)S(1)}, u32[]{:S(2)}, u32[]{:S(2)}) async-start(f32[4,64,512]{2,1,0:T(8,128)} %get-tuple-element.35), calls=%async_computation | async-start | bytes 1048576 | tf_op jit(solution)/shard_map/all_to_all | solution.py:151
  9.8 11.4 %collective-permute-start = (f32[2,64,512]{2,1,0:T(8,128)}, f32[2,64,512]{2,1,0:T(8,128)S(1)}, u32[]{:S(2)}, u32[]{:S(2)}) collective-permute-start(f32[2,64,512]{2,1,0:T(8,128)} %get-tuple-element.36), channel_id=1, source_target_pairs={{0,1},{1,2},{2,3},{3,4},{4,5},{5,6},{6,7},{7,0},{8,9},{9,10},{10,1... | collective-permute-start | bytes 786440 | tf_op jit(solution)/shard_map/ppermute | solution.py:128
  11.4 9.8 %collective-permute-start.1 = (f32[2,64,512]{2,1,0:T(8,128)}, f32[2,64,512]{2,1,0:T(8,128)S(1)}, u32[]{:S(2)}, u32[]{:S(2)}) collective-permute-start(f32[2,64,512]{2,1,0:T(8,128)} %get-tuple-element.37), channel_id=1, source_target_pairs={{0,7},{1,0},{2,1},{3,2},{4,3},{5,4},{6,5},{7,6},{8,15},{9,8},{10,9... | collective-permute-start | bytes 786440 | tf_op jit(solution)/shard_map/ppermute | solution.py:128
  22.5 10.2 %copy-start.6 = (s32[1,256]{1,0:T(1,128)S(1)}, s32[1,256]{1,0:T(1,128)}, u32[]{:S(2)}) copy-start(s32[1,256]{1,0:T(1,128)} %param.11) | copy-start | bytes 3076
  22.5 18.8 %copy-start.3 = (f32[4,64,512]{2,1,0:T(8,128)S(1)}, f32[4,64,512]{2,1,0:T(8,128)}, u32[]{:S(2)}) copy-start(f32[4,64,512]{2,1,0:T(8,128)} %get-tuple-element.44) | copy-start | bytes 1572868
  23.4 20.1 %copy-start.2 = (f32[4,64,512]{2,1,0:T(8,128)S(1)}, f32[4,64,512]{2,1,0:T(8,128)}, u32[]{:S(2)}) copy-start(f32[4,64,512]{2,1,0:T(8,128)} %get-tuple-element.46) | copy-start | bytes 1572868
  23.4 17.9 %collective-permute-start.2 = (f32[4,64,512]{2,1,0:T(8,128)}, f32[4,64,512]{2,1,0:T(8,128)S(1)}, u32[]{:S(2)}, u32[]{:S(2)}) collective-permute-start(f32[4,64,512]{2,1,0:T(8,128)} %pad_maximum_fusion), channel_id=1, source_target_pairs={{0,1},{1,2},{2,3},{3,4},{4,5},{5,6},{6,7},{7,0},{8,9},{9,10},{10,1... | collective-permute-start | bytes 1572872 | tf_op jit(solution)/shard_map/ppermute | solution.py:128
  24.2 17.0 %collective-permute-start.3 = (f32[4,64,512]{2,1,0:T(8,128)}, f32[4,64,512]{2,1,0:T(8,128)S(1)}, u32[]{:S(2)}, u32[]{:S(2)}) collective-permute-start(f32[4,64,512]{2,1,0:T(8,128)} %pad_maximum_fusion.1), channel_id=1, source_target_pairs={{0,7},{1,0},{2,1},{3,2},{4,3},{5,4},{6,5},{7,6},{8,15},{9,8},{10,9... | collective-permute-start | bytes 1572872 | tf_op jit(solution)/shard_map/ppermute | solution.py:128
  27.6 32.0 %copy-start.1 = (f32[4,64,512]{2,1,0:T(8,128)S(1)}, f32[4,64,512]{2,1,0:T(8,128)}, u32[]{:S(2)}) copy-start(f32[4,64,512]{2,1,0:T(8,128)} %get-tuple-element.49) | copy-start | bytes 1572868
  27.6 13.7 %all-to-all-start.1 = ((f32[8,8,512]{2,1,0:T(8,128)}), f32[8,8,512]{2,1,0:T(8,128)S(1)}, u32[]{:S(2)}, u32[]{:S(2)}) async-start(f32[8,8,512]{2,1,0:T(8,128)} %bitcast.2), calls=%async_computation.1 | async-start | bytes 262144 | tf_op jit(solution)/shard_map/all_to_all | solution.py:151
  42.2 18.8 %copy-start = (f32[4,64,512]{2,1,0:T(8,128)S(1)}, f32[4,64,512]{2,1,0:T(8,128)}, u32[]{:S(2)}) copy-start(f32[4,64,512]{2,1,0:T(8,128)} %get-tuple-element.51) | copy-start | bytes 1572868
  42.2 17.4 %collective-permute-start.4 = (f32[4,64,512]{2,1,0:T(8,128)}, f32[4,64,512]{2,1,0:T(8,128)S(1)}, u32[]{:S(2)}, u32[]{:S(2)}) collective-permute-start(f32[4,64,512]{2,1,0:T(8,128)} %add.54), channel_id=1, source_target_pairs={{0,1},{1,2},{2,3},{3,4},{4,5},{5,6},{6,7},{7,0},{8,9},{9,10},{10,1... | collective-permute-start | bytes 1572872 | tf_op jit(solution)/shard_map/ppermute | solution.py:128
  43.6 16.1 %collective-permute-start.5 = (f32[4,64,512]{2,1,0:T(8,128)S(1)}, f32[4,64,512]{2,1,0:T(8,128)S(1)}, u32[]{:S(2)}, u32[]{:S(2)}) collective-permute-start(f32[4,64,512]{2,1,0:T(8,128)S(1)} %add.55), channel_id=1, source_target_pairs={{0,7},{1,0},{2,1},{3,2},{4,3},{5,4},{6,5},{7,6},{8,15},{9,8},{10,9... | collective-permute-start | bytes 1572872 | tf_op jit(solution)/shard_map/ppermute | solution.py:128
  46.1 13.5 %all-to-all-start.2 = ((f32[8,8,512]{2,1,0:T(8,128)}), f32[8,8,512]{2,1,0:T(8,128)S(1)}, u32[]{:S(2)}, u32[]{:S(2)}) async-start(f32[8,8,512]{2,1,0:T(8,128)} %broadcast_in_dim.22), calls=%async_computation.2 | async-start | bytes 262144 | tf_op jit(solution)/shard_map/all_to_all | solution.py:151
  59.7 16.8 %collective-permute-start.6 = (f32[4,64,512]{2,1,0:T(8,128)S(1)}, f32[4,64,512]{2,1,0:T(8,128)S(1)}, u32[]{:S(2)}, u32[]{:S(2)}) collective-permute-start(f32[4,64,512]{2,1,0:T(8,128)S(1)} %add.56), channel_id=1, source_target_pairs={{0,1},{1,2},{2,3},{3,4},{4,5},{5,6},{6,7},{7,0},{8,9},{9,10},{10,1... | collective-permute-start | bytes 1572872 | tf_op jit(solution)/shard_map/ppermute | solution.py:128
  61.1 20.4 %copy-start.5 = (f32[4,64,512]{2,1,0:T(8,128)S(1)}, f32[4,64,512]{2,1,0:T(8,128)}, u32[]{:S(2)}) copy-start(f32[4,64,512]{2,1,0:T(8,128)} %get-tuple-element.34) | copy-start | bytes 1572868
  61.1 15.4 %collective-permute-start.7 = (f32[4,64,512]{2,1,0:T(8,128)S(1)}, f32[4,64,512]{2,1,0:T(8,128)S(1)}, u32[]{:S(2)}, u32[]{:S(2)}) collective-permute-start(f32[4,64,512]{2,1,0:T(8,128)S(1)} %add.57), channel_id=1, source_target_pairs={{0,7},{1,0},{2,1},{3,2},{4,3},{5,4},{6,5},{7,6},{8,15},{9,8},{10,9... | collective-permute-start | bytes 1572872 | tf_op jit(solution)/shard_map/ppermute | solution.py:128
  77.5 13.3 %all-to-all-start.4 = ((f32[4,64,768]{2,1,0:T(8,128)}), f32[4,64,768]{2,1,0:T(8,128)S(1)}, u32[]{:S(2)}, u32[]{:S(2)}) async-start(f32[4,64,768]{2,1,0:T(8,128)} %broadcast_in_dim.25), calls=%async_computation.4 | async-start | bytes 1572864 | tf_op jit(solution)/shard_map/all_to_all | solution.py:151
  81.5 15.7 %copy-start.4 = (f32[64,512]{1,0:T(8,128)S(1)}, f32[64,512]{1,0:T(8,128)}, u32[]{:S(2)}) copy-start(f32[64,512]{1,0:T(8,128)} %slab_ref.1) | copy-start | bytes 393220
  81.7 9.1 %collective-permute-start.8 = (f32[32,512]{1,0:T(8,128)S(1)}, f32[32,512]{1,0:T(8,128)S(1)}, u32[]{:S(2)}, u32[]{:S(2)}) collective-permute-start(f32[32,512]{1,0:T(8,128)S(1)} %get-tuple-element.68), channel_id=1, source_target_pairs={{0,8},{8,16},{16,24},{24,0},{1,9},{9,17},{17,25},{25,1},{2,10},{10... | collective-permute-start | bytes 196616 | tf_op jit(solution)/shard_map/ppermute | solution.py:128
  83.3 7.5 %collective-permute-start.9 = (f32[32,512]{1,0:T(8,128)S(1)}, f32[32,512]{1,0:T(8,128)S(1)}, u32[]{:S(2)}, u32[]{:S(2)}) collective-permute-start(f32[32,512]{1,0:T(8,128)S(1)} %get-tuple-element.67), channel_id=1, source_target_pairs={{0,24},{8,0},{16,8},{24,16},{1,25},{9,1},{17,9},{25,17},{2,26},{10... | collective-permute-start | bytes 196616 | tf_op jit(solution)/shard_map/ppermute | solution.py:128
  90.8 4.6 %collective-permute-start.11 = (f32[64,512]{1,0:T(8,128)S(1)}, f32[64,512]{1,0:T(8,128)S(1)}, u32[]{:S(2)}, u32[]{:S(2)}) collective-permute-start(f32[64,512]{1,0:T(8,128)S(1)} %pad_maximum_fusion.3), channel_id=1, source_target_pairs={{0,24},{8,0},{16,8},{24,16},{1,25},{9,1},{17,9},{25,17},{2,26},{10... | collective-permute-start | bytes 393224 | tf_op jit(solution)/shard_map/ppermute | solution.py:128
  92.1 5.1 %collective-permute-start.10 = (f32[64,512]{1,0:T(8,128)S(1)}, f32[64,512]{1,0:T(8,128)S(1)}, u32[]{:S(2)}, u32[]{:S(2)}) collective-permute-start(f32[64,512]{1,0:T(8,128)S(1)} %pad_maximum_fusion.2), channel_id=1, source_target_pairs={{0,8},{8,16},{16,24},{24,0},{1,9},{9,17},{17,25},{25,1},{2,10},{10... | collective-permute-start | bytes 393224 | tf_op jit(solution)/shard_map/ppermute | solution.py:128
  98.9 25.5 %all-to-all-start.5 = ((f32[8,64,512]{2,1,0:T(8,128)}), f32[8,64,512]{2,1,0:T(8,128)S(1)}, u32[]{:S(2)}, u32[]{:S(2)}) async-start(f32[8,64,512]{2,1,0:T(8,128)} %broadcast_in_dim.26), calls=%async_computation.5 | async-start | bytes 2097152 | tf_op jit(solution)/shard_map/slab_swap/all_to_all | solution.py:151

commit v2 on v1

--- a/solution.py
+++ b/solution.py
@@ -42,8 +42,8 @@
 
 
 def scatter_kernel(tc_ref, tr_ref, lr_ref, blocks_ref, slab_ref, pan_out, *rest):
-    dense_outs = rest[:9]
-    tc, tr, lr, own, buf, dense, pan, in_sem, num_sem, out_sem = rest[9:]
+    dense_outs = rest[:NZ]
+    tc, tr, lr, own, buf, dense, pan, in_sem, num_sem, out_sem = rest[NZ:]
     my_x = lax.axis_index(AX)
     my_z = lax.axis_index(AZ)
     owner = (my_x == 0) & (my_z < OWNERS)
@@ -102,12 +102,12 @@
 
 
 def scatter(tc, tr, lr, blocks, slab):
-    sizes = [NX] * 4 + [NX // 2] * 2 + [NX] * 3
+    sizes = [NX] * NZ
     outs = pl.pallas_call(
         scatter_kernel,
         out_shape=[jax.ShapeDtypeStruct((n, NB, ROWS_DEV), F32) for n in [OWNERS] + sizes],
         in_specs=[HBM] * 5,
-        out_specs=[HBM] * 10,
+        out_specs=[HBM] * (1 + NZ),
         scratch_shapes=[pltpu.SMEM((1, CB_DEV), jnp.int32)] * 3
         + [
             pltpu.VMEM((NB, ROWS_DEV), F32),
@@ -116,7 +116,7 @@
             pltpu.VMEM((OWNERS, NB, ROWS_DEV), F32),
             pltpu.SemaphoreType.DMA((CB_DEV // CH,)),
             pltpu.SemaphoreType.DMA((4,)),
-            pltpu.SemaphoreType.DMA((10,)),
+            pltpu.SemaphoreType.DMA((1 + NZ,)),
         ],
         compiler_params=pltpu.CompilerParams(vmem_limit_bytes=56 * MIB),
         name="scatter",
@@ -128,32 +128,32 @@
     return lax.ppermute(value, axis, [(i, (i + step) % n) for i in range(n)])
 
 
-def ring_sum(rel, halves, axis, n):
-    h = halves[0].shape[0]
-    pair = yield shift(halves[0], axis, n, 1), shift(halves[1], axis, n, -1)
+def ring_sum(rel, axis, n):
+    ahead, back = yield [shift(rel[n // 2], axis, n, 1), shift(rel[n // 2 + 1], axis, n, -1)]
     for d in range(n // 2 - 1, 0, -1):
-        up, down = rel[d], rel[n - d]
-        if d == n // 2 - 1:
-            up = jnp.concatenate([up[:h] + pair[0], up[h:]], axis=0)
-            down = jnp.concatenate([down[:h], down[h:] + pair[1]], axis=0)
+        sent = [shift(rel[d] + ahead, axis, n, 1)]
+        if d > 1:
+            sent.append(shift(rel[n - d + 1] + back, axis, n, -1))
+            ahead, back = yield sent
         else:
-            up, down = up + pair[0], down + pair[1]
-        pair = yield shift(up, axis, n, 1), shift(down, axis, n, -1)
-    yield rel[0] + pair[0] + pair[1]
-
-
-def tied(value, pair):
-    value, first, second = lax.optimization_barrier((value, *pair))
-    return value, (first, second)
+            (ahead,) = yield sent
+    yield rel[0] + back + ahead
+
+
+def tied(value, sent):
+    return value, lax.optimization_barrier((value, *sent))[1:]
 
 
 def exchange(value, axis):
     return lax.all_to_all(value, axis, split_axis=0, concat_axis=0, tiled=True)
 
 
+def copied(value, n):
+    return jnp.broadcast_to(value, (n, *value.shape))
+
+
 def gather(value, axis, n):
-    copies = jnp.broadcast_to(value, (n, *value.shape))
-    return exchange(copies, axis)
+    return exchange(copied(value, n), axis)
 
 
 def factor_kernel(t_ref, packed_ref, loinv_ref, upinv_ref, x_ref, v_ref, r_ref, lo_ref, ti_ref, b_ref):
@@ -282,27 +282,26 @@
     pick = (pivot[:, None] == row_group * ROWS_DEV + jnp.arange(ROWS_DEV)[None, :]).astype(F32)
     hit = jnp.sum(pick, axis=0) > 0
 
-    along_z = ring_sum(dense[:4] + [None] + dense[6:], (dense[4], dense[5]), AZ, NZ)
+    along_z = ring_sum(dense, AZ, NZ)
     pair = next(along_z)
-    chunk, pair = tied(exchange(pan, AX), pair)
-    pair = along_z.send(pair)
-    chunk = exchange(chunk.sum(axis=0).reshape(NZ, NB // NZ, ROWS_DEV), AZ)
+    chunk = exchange(pan, AX).sum(axis=0).reshape(NZ, NB // NZ, ROWS_DEV)
     chunk, pair = tied(chunk, pair)
     pair = along_z.send(pair)
-    chunk = chunk.sum(axis=0)
+    chunk = exchange(chunk, AZ).sum(axis=0)
     offer = jnp.concatenate([dot_nt(chunk, pick), chunk[:, :PW]], axis=1)
-    offers, pair = tied(gather(offer, AY, PROW), pair)
+    offers, pair = tied(copied(offer, PROW), pair)
     pair = along_z.send(pair)
+    offers = exchange(offers, AY)
     moved = offers[0, :, PW:]
     chunk = jnp.where(hit[None, :], dotf(moved, pick), chunk)
     both = jnp.concatenate([offers[:, :, :PW].sum(axis=0), chunk], axis=1)
-    both, pair = tied(gather(both, AZ, NZ), pair)
-    part = along_z.send(pair)
-    half = part[NX // 2]
-    along_x = ring_sum([part[0], part[1], None, part[3]], (half[: NB // 2], half[NB // 2 :]), AX, NX)
+    both = exchange(copied(both, NZ), AZ).reshape(NB, PW + ROWS_DEV)
+    both, pair = tied(both, pair)
+    pair = along_z.send(pair)
+    both, pair = tied(copied(both, NX), pair)
+    along_x = ring_sum(along_z.send(pair), AX, NX)
     pair = next(along_x)
-    both, pair = tied(gather(both.reshape(NB, PW + ROWS_DEV), AX, NX), pair)
-    both = both.reshape(PW, PW + ROWS_DEV)
+    both, pair = tied(exchange(both, AX).reshape(PW, PW + ROWS_DEV), pair)
     pair = along_x.send(pair)
     matrix = matrix_slab + along_x.send(pair)
     with jax.named_scope("slab_swap"):

time: 127 us -> 120 us (0.945)
  waiting for transfers between devices: 30.5 us -> 24.9 us
  other arithmetic: 5.25 us -> 3.09 us
  blocking collectives: 13.5 us -> 15.4 us
  starting transfers between devices: 50.5 us -> 48.9 us
    ppermute x12 -> x10, starting transfers between devices: 18.3 us -> 14.3 us  [shift(): return lax.ppermute(value, axis, [(i, (i + step) % n) for i in range(n)])]
    ppermute x12 -> x10, waiting for transfers between devices: 16.9 us -> 13.4 us  [shift(): return lax.ppermute(value, axis, [(i, (i + step) % n) for i in range(n)])]
    all_to_all x5, starting transfers between devices: 32.2 us -> 34.5 us  [exchange(): return lax.all_to_all(value, axis, split_axis=0, concat_axis=0, tiled=True)]
    all_to_all x5, waiting for transfers between devices: 13.6 us -> 11.5 us  [exchange(): return lax.all_to_all(value, axis, split_axis=0, concat_axis=0, tiled=True)]
    all_to_all x1, blocking collectives: 13.5 us -> 15.4 us  [exchange(): return lax.all_to_all(value, axis, split_axis=0, concat_axis=0, tiled=True)]
    concatenate x4 -> x0, other arithmetic: 1.69 us -> none  [the longest x2 0.85 us: ring_sum(): up = jnp.concatenate([up[:h] + pair[0], up[h:]], axis=0)]
  transfers between devices with their start and end apart: 17 -> 15, of which waited for: 6 -> 7; matrix products, arithmetic and copies ran while one was open for 3% -> 5% of each run, Pallas kernels for 12% -> 13%
where the time goes in v2:
time: 120 us; the launch traced here: 119 us
  starting transfers between devices  48.9 us (41%)
  waiting for transfers between devices  24.9 us (21%)
  Pallas kernels  22.4 us (19%)
  blocking collectives  15.4 us (13%)
  other arithmetic  3.09 us (3%)
  local copies, waits for them, and re-layouts  3.01 us (3%)
    all_to_all x5, starting transfers between devices, exchange(): return lax.all_to_all(value, axis, split_axis=0, concat_axis=0, tiled=True)  34.5 us
    pallas_call x1, Pallas kernels, factor(): pl.pallas_call(factor_kernel, out_shape=[jax.ShapeDtypeStruct((PW, PW), F...  15.4 us
    all_to_all x1, blocking collectives, exchange(): return lax.all_to_all(value, axis, split_axis=0, concat_axis=0, tiled=True)  15.4 us
    ppermute x10, starting transfers between devices, shift(): return lax.ppermute(value, axis, [(i, (i + step) % n) for i in range(n)])  14.3 us
    ppermute x10, waiting for transfers between devices, shift(): return lax.ppermute(value, axis, [(i, (i + step) % n) for i in range(n)])  13.4 us
    all_to_all x5, waiting for transfers between devices, exchange(): return lax.all_to_all(value, axis, split_axis=0, concat_axis=0, tiled=True)  11.5 us
    pallas_call x1, Pallas kernels, scatter(): pl.pallas_call(scatter_kernel, out_shape=[jax.ShapeDtypeStruct((n, NB, RO...  4.88 us
    broadcast_in_dim x4, local copies, waits for them, and re-layouts, copied(): return jnp.broadcast_to(value, (n, *value.shape))  2.74 us
  transfers between devices with their start and end apart: 15, of which 7 were waited for; matrix products, arithmetic and copies ran while one was open for 5% of the time, Pallas kernels for 13%

profile of v2, /device:TPU:1, one launch (start us, length us, event | category | flops | bytes accessed | tf_op | source)
XLA Modules:
  0.0 119.0 jit_solution(17320638765871954219)
XLA Ops:
  0.0 4.9 %scatter.1 = (f32[4,64,512]{2,1,0:T(8,128)}, f32[4,64,512]{2,1,0:T(8,128)}, f32[4,64,512]{2,1,0:T(8,128)}, f32[4,64,512]{2,1,0:T(8,128)}, f32[4,64,512]{2,1,0:T(...) custom-call(s32[1,32]{1,0:T(1,128)} %tc_ref.1, ...), custom_call_target="tpu_custom_call" | custom-call | tf_op jit(solution)/shard_map/scatter/pallas_call | solution.py:106
  4.9 5.0 %all-to-all-start = ((f32[4,64,512]{2,1,0:T(8,128)}), f32[4,64,512]{2,1,0:T(8,128)S(1)}, u32[]{:S(2)}, u32[]{:S(2)}) async-start(f32[4,64,512]{2,1,0:T(8,128)} %get-tuple-element.28), calls=%async_computation | async-start | bytes 1048576 | tf_op jit(solution)/shard_map/all_to_all | solution.py:148
  9.9 1.6 %collective-permute-start = (f32[4,64,512]{2,1,0:T(8,128)}, f32[4,64,512]{2,1,0:T(8,128)S(1)}, u32[]{:S(2)}, u32[]{:S(2)}) collective-permute-start(f32[4,64,512]{2,1,0:T(8,128)} %get-tuple-element.31), channel_id=1, source_target_pairs={{0,1},{1,2},{2,3},{3,4},{4,5},{5,6},{6,7},{7,0},{8,9},{9,10},{10,1... | collective-permute-start | bytes 1572872 | tf_op jit(solution)/shard_map/ppermute | solution.py:128
  11.5 3.9 %collective-permute-start.1 = (f32[4,64,512]{2,1,0:T(8,128)}, f32[4,64,512]{2,1,0:T(8,128)S(1)}, u32[]{:S(2)}, u32[]{:S(2)}) collective-permute-start(f32[4,64,512]{2,1,0:T(8,128)} %get-tuple-element.32), channel_id=1, source_target_pairs={{0,7},{1,0},{2,1},{3,2},{4,3},{5,4},{6,5},{7,6},{8,15},{9,8},{10,9... | collective-permute-start | bytes 1572872 | tf_op jit(solution)/shard_map/ppermute | solution.py:128
  15.5 1.8 %all-to-all-done = f32[4,64,512]{2,1,0:T(8,128)S(1)} async-done(((f32[4,64,512]{2,1,0:T(8,128)}), f32[4,64,512]{2,1,0:T(8,128)S(1)}, u32[]{:S(2)}, u32[]{:S(2)}) %all-to-all-start) | async-done | bytes 524320 | tf_op jit(solution)/shard_map/all_to_all | solution.py:148
  17.3 0.7 reduce_sum.36
  18.0 9.1 %all-to-all-start.1 = ((f32[8,8,512]{2,1,0:T(8,128)}), f32[8,8,512]{2,1,0:T(8,128)S(1)}, u32[]{:S(2)}, u32[]{:S(2)}) async-start(f32[8,8,512]{2,1,0:T(8,128)} %bitcast.2), calls=%async_computation.1 | async-start | bytes 262144 | tf_op jit(solution)/shard_map/all_to_all | solution.py:148
  27.3 0.9 add.47
  28.1 2.7 %collective-permute-start.3 = (f32[4,64,512]{2,1,0:T(8,128)}, f32[4,64,512]{2,1,0:T(8,128)S(1)}, u32[]{:S(2)}, u32[]{:S(2)}) collective-permute-start(f32[4,64,512]{2,1,0:T(8,128)} %add.47), channel_id=1, source_target_pairs={{0,7},{1,0},{2,1},{3,2},{4,3},{5,4},{6,5},{7,6},{8,15},{9,8},{10,9... | collective-permute-start | bytes 1572872 | tf_op jit(solution)/shard_map/ppermute | solution.py:128
  30.8 0.9 add.46
  31.7 3.4 %all-to-all-done.1 = f32[8,8,512]{2,1,0:T(8,128)S(1)} async-done(((f32[8,8,512]{2,1,0:T(8,128)}), f32[8,8,512]{2,1,0:T(8,128)S(1)}, u32[]{:S(2)}, u32[]{:S(2)}) %all-to-all-start.1) | async-done | bytes 131104 | tf_op jit(solution)/shard_map/all_to_all | solution.py:148
  35.1 0.4 fusion.3
  35.5 0.7 broadcast_in_dim.22
  36.2 8.5 %all-to-all-start.2 = ((f32[8,8,512]{2,1,0:T(8,128)}), f32[8,8,512]{2,1,0:T(8,128)S(1)}, u32[]{:S(2)}, u32[]{:S(2)}) async-start(f32[8,8,512]{2,1,0:T(8,128)} %broadcast_in_dim.22), calls=%async_computation.2 | async-start | bytes 262144 | tf_op jit(solution)/shard_map/all_to_all | solution.py:148
  44.7 5.3 %all-to-all-done.2 = f32[8,8,512]{2,1,0:T(8,128)S(1)} async-done(((f32[8,8,512]{2,1,0:T(8,128)}), f32[8,8,512]{2,1,0:T(8,128)S(1)}, u32[]{:S(2)}, u32[]{:S(2)}) %all-to-all-start.2) | async-done | bytes 131104 | tf_op jit(solution)/shard_map/all_to_all | solution.py:148
  50.8 1.3 %collective-permute-start.4 = (f32[4,64,512]{2,1,0:T(8,128)S(1)}, f32[4,64,512]{2,1,0:T(8,128)S(1)}, u32[]{:S(2)}, u32[]{:S(2)}) collective-permute-start(f32[4,64,512]{2,1,0:T(8,128)S(1)} %add.48), channel_id=1, source_target_pairs={{0,1},{1,2},{2,3},{3,4},{4,5},{5,6},{6,7},{7,0},{8,9},{9,10},{10,1... | collective-permute-start | bytes 1572872 | tf_op jit(solution)/shard_map/ppermute | solution.py:128
  52.1 15.4 %all_to_all.30 = f32[8,8,768]{2,1,0:T(8,128)S(1)} all-to-all(f32[8,8,768]{2,1,0:T(8,128)S(1)} %broadcast_in_dim.24), channel_id=1, replica_groups=mesh['prow'=8,'pcol_0'=4,'pcol_1'=8] {'pcol_1'}, dimensions={0} | all-to-all | bytes 393216 | tf_op jit(solution)/shard_map/all_to_all | solution.py:148
  67.6 0.8 collective-permute-start.6
  68.4 0.9 broadcast_in_dim.25
  69.4 4.5 %all-to-all-start.4 = ((f32[4,64,768]{2,1,0:T(8,128)}), f32[4,64,768]{2,1,0:T(8,128)S(1)}, u32[]{:S(2)}, u32[]{:S(2)}) async-start(f32[4,64,768]{2,1,0:T(8,128)} %broadcast_in_dim.25), calls=%async_computation.4 | async-start | bytes 1572864 | tf_op jit(solution)/shard_map/all_to_all | solution.py:148
  73.8 5.4 %collective-permute-done.6 = f32[4,64,512]{2,1,0:T(8,128)S(1)} collective-permute-done((f32[4,64,512]{2,1,0:T(8,128)S(1)}, f32[4,64,512]{2,1,0:T(8,128)S(1)}, u32[]{:S(2)}, u32[]{:S(2)}) %collective-permute-start.6) | collective-permute-done | bytes 524320 | tf_op jit(solution)/shard_map/ppermute | solution.py:128
  79.4 1.5 %collective-permute-start.7 = (f32[64,512]{1,0:T(8,128)S(1)}, f32[64,512]{1,0:T(8,128)S(1)}, u32[]{:S(2)}, u32[]{:S(2)}) collective-permute-start(f32[64,512]{1,0:T(8,128)S(1)} %get-tuple-element.50), channel_id=1, source_target_pairs={{0,8},{8,16},{16,24},{24,0},{1,9},{9,17},{17,25},{25,1},{2,10},{10... | collective-permute-start | bytes 393224 | tf_op jit(solution)/shard_map/ppermute | solution.py:128
  80.9 1.2 %collective-permute-start.8 = (f32[64,512]{1,0:T(8,128)S(1)}, f32[64,512]{1,0:T(8,128)S(1)}, u32[]{:S(2)}, u32[]{:S(2)}) collective-permute-start(f32[64,512]{1,0:T(8,128)S(1)} %get-tuple-element.49), channel_id=1, source_target_pairs={{0,24},{8,0},{16,8},{24,16},{1,25},{9,1},{17,9},{25,17},{2,26},{10... | collective-permute-start | bytes 393224 | tf_op jit(solution)/shard_map/ppermute | solution.py:128
  82.1 1.0 all-to-all-done.4
  83.1 3.8 %collective-permute-done.7 = f32[64,512]{1,0:T(8,128)S(1)} collective-permute-done((f32[64,512]{1,0:T(8,128)S(1)}, f32[64,512]{1,0:T(8,128)S(1)}, u32[]{:S(2)}, u32[]{:S(2)}) %collective-permute-start.7) | collective-permute-done | bytes 131104 | tf_op jit(solution)/shard_map/ppermute | solution.py:128
  87.0 0.9 collective-permute-start.9
  87.9 4.2 %collective-permute-done.9 = f32[64,512]{1,0:T(8,128)S(1)} collective-permute-done((f32[64,512]{1,0:T(8,128)S(1)}, f32[64,512]{1,0:T(8,128)S(1)}, u32[]{:S(2)}, u32[]{:S(2)}) %collective-permute-start.9) | collective-permute-done | bytes 131104 | tf_op jit(solution)/shard_map/ppermute | solution.py:128
  92.1 0.4 fusion
  92.6 1.1 broadcast_in_dim.26
  93.7 7.5 %all-to-all-start.5 = ((f32[8,64,512]{2,1,0:T(8,128)}), f32[8,64,512]{2,1,0:T(8,128)S(1)}, u32[]{:S(2)}, u32[]{:S(2)}) async-start(f32[8,64,512]{2,1,0:T(8,128)} %broadcast_in_dim.26), calls=%async_computation.5 | async-start | bytes 2097152 | tf_op jit(solution)/shard_map/slab_swap/all_to_all | solution.py:148
  101.5 15.4 %factor.1 = (f32[256,256]{1,0:T(8,128)S(1)}, f32[256,256]{1,0:T(8,128)S(1)}, f32[256,256]{1,0:T(8,128)S(1)}) custom-call(f32[256,256]{1,0:T(8,128)S(1)} %slice.49.t_ref), custom_call_target="tpu_custom_call" | custom-call | flops 40000000 | bytes 60000000 | tf_op jit(solution)/shard_map/factor/pallas_call | solution.py:226
  116.9 2.1 %finish.1 = f32[64,512]{1,0:T(8,128)} custom-call(s32[256,1]{1,0:T(8,128)S(1)} %copy.8.pivot_ref, f32[64,512]{1,0:T(8,128)S(1)} %fusion.15.matrix_ref, f32[8,64,512]{2,1,0:T(8,128)S(1)} %all-to-all-done.5.offers_ref, f32[256,512]{1,0:T(8,128)S(1)} %slice.48.panel_ref, f32[256,256]{1,0:T(8,128)S(1)} %get-tuple-element.46.packed_ref, ...), custom_call_target="tpu_custom_call" | custom-call | tf_op jit(solution)/shard_map/finish/pallas_call | solution.py:267
  (48 shorter events, 1.6 us)
Async XLA Ops:
  0.0 27.1 %copy-start.7 = (s32[1,256]{1,0:T(1,128)S(1)}, s32[1,256]{1,0:T(1,128)}, u32[]{:S(2)}) copy-start(s32[1,256]{1,0:T(1,128)} %param.11) | copy-start | bytes 3076
  4.9 22.4 %copy-start.4 = (f32[4,64,512]{2,1,0:T(8,128)S(1)}, f32[4,64,512]{2,1,0:T(8,128)}, u32[]{:S(2)}) copy-start(f32[4,64,512]{2,1,0:T(8,128)} %get-tuple-element.34) | copy-start | bytes 1572868
  4.9 25.9 %copy-start.3 = (f32[4,64,512]{2,1,0:T(8,128)S(1)}, f32[4,64,512]{2,1,0:T(8,128)}, u32[]{:S(2)}) copy-start(f32[4,64,512]{2,1,0:T(8,128)} %get-tuple-element.30) | copy-start | bytes 1572868
  4.9 12.4 %all-to-all-start = ((f32[4,64,512]{2,1,0:T(8,128)}), f32[4,64,512]{2,1,0:T(8,128)S(1)}, u32[]{:S(2)}, u32[]{:S(2)}) async-start(f32[4,64,512]{2,1,0:T(8,128)} %get-tuple-element.28), calls=%async_computation | async-start | bytes 1048576 | tf_op jit(solution)/shard_map/all_to_all | solution.py:148
  9.9 17.3 %collective-permute-start = (f32[4,64,512]{2,1,0:T(8,128)}, f32[4,64,512]{2,1,0:T(8,128)S(1)}, u32[]{:S(2)}, u32[]{:S(2)}) collective-permute-start(f32[4,64,512]{2,1,0:T(8,128)} %get-tuple-element.31), channel_id=1, source_target_pairs={{0,1},{1,2},{2,3},{3,4},{4,5},{5,6},{6,7},{7,0},{8,9},{9,10},{10,1... | collective-permute-start | bytes 1572872 | tf_op jit(solution)/shard_map/ppermute | solution.py:128
  11.5 15.7 %collective-permute-start.1 = (f32[4,64,512]{2,1,0:T(8,128)}, f32[4,64,512]{2,1,0:T(8,128)S(1)}, u32[]{:S(2)}, u32[]{:S(2)}) collective-permute-start(f32[4,64,512]{2,1,0:T(8,128)} %get-tuple-element.32), channel_id=1, source_target_pairs={{0,7},{1,0},{2,1},{3,2},{4,3},{5,4},{6,5},{7,6},{8,15},{9,8},{10,9... | collective-permute-start | bytes 1572872 | tf_op jit(solution)/shard_map/ppermute | solution.py:128
  18.0 17.1 %all-to-all-start.1 = ((f32[8,8,512]{2,1,0:T(8,128)}), f32[8,8,512]{2,1,0:T(8,128)S(1)}, u32[]{:S(2)}, u32[]{:S(2)}) async-start(f32[8,8,512]{2,1,0:T(8,128)} %bitcast.2), calls=%async_computation.1 | async-start | bytes 262144 | tf_op jit(solution)/shard_map/all_to_all | solution.py:148
  27.1 23.2 %copy-start.2 = (f32[4,64,512]{2,1,0:T(8,128)S(1)}, f32[4,64,512]{2,1,0:T(8,128)}, u32[]{:S(2)}) copy-start(f32[4,64,512]{2,1,0:T(8,128)} %get-tuple-element.37) | copy-start | bytes 1572868
  28.1 22.6 %copy-start.1 = (f32[4,64,512]{2,1,0:T(8,128)S(1)}, f32[4,64,512]{2,1,0:T(8,128)}, u32[]{:S(2)}) copy-start(f32[4,64,512]{2,1,0:T(8,128)} %get-tuple-element.29) | copy-start | bytes 1572868
  28.1 22.1 %collective-permute-start.3 = (f32[4,64,512]{2,1,0:T(8,128)}, f32[4,64,512]{2,1,0:T(8,128)S(1)}, u32[]{:S(2)}, u32[]{:S(2)}) collective-permute-start(f32[4,64,512]{2,1,0:T(8,128)} %add.47), channel_id=1, source_target_pairs={{0,7},{1,0},{2,1},{3,2},{4,3},{5,4},{6,5},{7,6},{8,15},{9,8},{10,9... | collective-permute-start | bytes 1572872 | tf_op jit(solution)/shard_map/ppermute | solution.py:128
  31.7 18.6 %collective-permute-start.2 = (f32[4,64,512]{2,1,0:T(8,128)}, f32[4,64,512]{2,1,0:T(8,128)S(1)}, u32[]{:S(2)}, u32[]{:S(2)}) collective-permute-start(f32[4,64,512]{2,1,0:T(8,128)} %add.46), channel_id=1, source_target_pairs={{0,1},{1,2},{2,3},{3,4},{4,5},{5,6},{6,7},{7,0},{8,9},{9,10},{10,1... | collective-permute-start | bytes 1572872 | tf_op jit(solution)/shard_map/ppermute | solution.py:128
  36.2 31.3 %copy-start = (f32[4,64,512]{2,1,0:T(8,128)S(1)}, f32[4,64,512]{2,1,0:T(8,128)}, u32[]{:S(2)}) copy-start(f32[4,64,512]{2,1,0:T(8,128)} %get-tuple-element.40) | copy-start | bytes 1572868
  36.2 13.8 %all-to-all-start.2 = ((f32[8,8,512]{2,1,0:T(8,128)}), f32[8,8,512]{2,1,0:T(8,128)S(1)}, u32[]{:S(2)}, u32[]{:S(2)}) async-start(f32[8,8,512]{2,1,0:T(8,128)} %broadcast_in_dim.22), calls=%async_computation.2 | async-start | bytes 262144 | tf_op jit(solution)/shard_map/all_to_all | solution.py:148
  50.4 17.1 %collective-permute-start.5 = (f32[4,64,512]{2,1,0:T(8,128)S(1)}, f32[4,64,512]{2,1,0:T(8,128)S(1)}, u32[]{:S(2)}, u32[]{:S(2)}) collective-permute-start(f32[4,64,512]{2,1,0:T(8,128)S(1)} %add.49), channel_id=1, source_target_pairs={{0,7},{1,0},{2,1},{3,2},{4,3},{5,4},{6,5},{7,6},{8,15},{9,8},{10,9... | collective-permute-start | bytes 1572872 | tf_op jit(solution)/shard_map/ppermute | solution.py:128
  50.8 16.7 %collective-permute-start.4 = (f32[4,64,512]{2,1,0:T(8,128)S(1)}, f32[4,64,512]{2,1,0:T(8,128)S(1)}, u32[]{:S(2)}, u32[]{:S(2)}) collective-permute-start(f32[4,64,512]{2,1,0:T(8,128)S(1)} %add.48), channel_id=1, source_target_pairs={{0,1},{1,2},{2,3},{3,4},{4,5},{5,6},{6,7},{7,0},{8,9},{9,10},{10,1... | collective-permute-start | bytes 1572872 | tf_op jit(solution)/shard_map/ppermute | solution.py:128
  67.5 11.7 %copy-start.6 = (f32[4,64,512]{2,1,0:T(8,128)S(1)}, f32[4,64,512]{2,1,0:T(8,128)}, u32[]{:S(2)}) copy-start(f32[4,64,512]{2,1,0:T(8,128)} %get-tuple-element.27) | copy-start | bytes 1572868
  67.6 11.6 %collective-permute-start.6 = (f32[4,64,512]{2,1,0:T(8,128)S(1)}, f32[4,64,512]{2,1,0:T(8,128)S(1)}, u32[]{:S(2)}, u32[]{:S(2)}) collective-permute-start(f32[4,64,512]{2,1,0:T(8,128)S(1)} %add.51), channel_id=1, source_target_pairs={{0,1},{1,2},{2,3},{3,4},{4,5},{5,6},{6,7},{7,0},{8,9},{9,10},{10,1... | collective-permute-start | bytes 1572872 | tf_op jit(solution)/shard_map/ppermute | solution.py:128
  69.3 22.7 %copy-start.5 = (f32[64,512]{1,0:T(8,128)S(1)}, f32[64,512]{1,0:T(8,128)}, u32[]{:S(2)}) copy-start(f32[64,512]{1,0:T(8,128)} %slab_ref.1) | copy-start | bytes 393220
  69.4 13.7 %all-to-all-start.4 = ((f32[4,64,768]{2,1,0:T(8,128)}), f32[4,64,768]{2,1,0:T(8,128)S(1)}, u32[]{:S(2)}, u32[]{:S(2)}) async-start(f32[4,64,768]{2,1,0:T(8,128)} %broadcast_in_dim.25), calls=%async_computation.4 | async-start | bytes 1572864 | tf_op jit(solution)/shard_map/all_to_all | solution.py:148
  79.4 7.6 %collective-permute-start.7 = (f32[64,512]{1,0:T(8,128)S(1)}, f32[64,512]{1,0:T(8,128)S(1)}, u32[]{:S(2)}, u32[]{:S(2)}) collective-permute-start(f32[64,512]{1,0:T(8,128)S(1)} %get-tuple-element.50), channel_id=1, source_target_pairs={{0,8},{8,16},{16,24},{24,0},{1,9},{9,17},{17,25},{25,1},{2,10},{10... | collective-permute-start | bytes 393224 | tf_op jit(solution)/shard_map/ppermute | solution.py:128
  80.9 6.0 %collective-permute-start.8 = (f32[64,512]{1,0:T(8,128)S(1)}, f32[64,512]{1,0:T(8,128)S(1)}, u32[]{:S(2)}, u32[]{:S(2)}) collective-permute-start(f32[64,512]{1,0:T(8,128)S(1)} %get-tuple-element.49), channel_id=1, source_target_pairs={{0,24},{8,0},{16,8},{24,16},{1,25},{9,1},{17,9},{25,17},{2,26},{10... | collective-permute-start | bytes 393224 | tf_op jit(solution)/shard_map/ppermute | solution.py:128
  87.0 5.1 %collective-permute-start.9 = (f32[64,512]{1,0:T(8,128)S(1)}, f32[64,512]{1,0:T(8,128)S(1)}, u32[]{:S(2)}, u32[]{:S(2)}) collective-permute-start(f32[64,512]{1,0:T(8,128)S(1)} %fusion.12), channel_id=1, source_target_pairs={{0,8},{8,16},{16,24},{24,0},{1,9},{9,17},{17,25},{25,1},{2,10},{10... | collective-permute-start | bytes 393224 | tf_op jit(solution)/shard_map/ppermute | solution.py:128
  93.7 23.2 %all-to-all-start.5 = ((f32[8,64,512]{2,1,0:T(8,128)}), f32[8,64,512]{2,1,0:T(8,128)S(1)}, u32[]{:S(2)}, u32[]{:S(2)}) async-start(f32[8,64,512]{2,1,0:T(8,128)} %broadcast_in_dim.26), calls=%async_computation.5 | async-start | bytes 2097152 | tf_op jit(solution)/shard_map/slab_swap/all_to_all | solution.py:148

commit v3 on v2

--- a/solution.py
+++ b/solution.py
@@ -41,87 +41,114 @@
 CH = 8
 
 
-def scatter_kernel(tc_ref, tr_ref, lr_ref, blocks_ref, slab_ref, pan_out, *rest):
-    dense_outs = rest[:NZ]
-    tc, tr, lr, own, buf, dense, pan, in_sem, num_sem, out_sem = rest[NZ:]
-    my_x = lax.axis_index(AX)
+def start_loads(sources, targets, sems):
+    copies = [pltpu.make_async_copy(src, dst, sems.at[i]) for i, (src, dst) in enumerate(zip(sources, targets))]
+    for copy in copies:
+        copy.start()
+    return copies
+
+
+def add_blocks(numbers, loads, buf, place):
+    tc, tr, lr = numbers
+    lane = lax.broadcasted_iota(jnp.int32, (NB, TR), 1)
+
+    def add(i, carry):
+        at = pl.ds(pl.multiple_of(tr[0, i] * TR, TR), TR)
+        place(tc[0, i], at, lambda: jnp.where(lane < lr[0, i], buf[i], 0.0))
+        return carry
+
+    for i in range(CB_DEV // CH):
+        loads[i].wait()
+        lax.fori_loop(i * CH, (i + 1) * CH, add, 0)
+
+
+def parts_of(ref):
+    return [ref.at[pl.ds(i * CH, CH)] for i in range(CB_DEV // CH)]
+
+
+def panel_kernel(tc_ref, tr_ref, lr_ref, blocks_ref, slab_ref, pan_out, tc, tr, lr, own, buf, pan, in_sem, num_sem, out_sem):
     my_z = lax.axis_index(AZ)
-    owner = (my_x == 0) & (my_z < OWNERS)
-    numbers = [
-        pltpu.make_async_copy(src, dst, num_sem.at[i])
-        for i, (src, dst) in enumerate(((tc_ref, tc), (tr_ref, tr), (lr_ref, lr), (slab_ref, own)))
-    ]
-    for number in numbers:
-        number.start()
-    loads = [
-        pltpu.make_async_copy(blocks_ref.at[pl.ds(i * CH, CH)], buf.at[pl.ds(i * CH, CH)], in_sem.at[i])
-        for i in range(CB_DEV // CH)
-    ]
-    for load in loads:
-        load.start()
-
-    def clear(i, carry):
-        dense[i] = jnp.zeros((NB, ROWS_DEV), F32)
-        return carry
-
-    lax.fori_loop(0, NX * NZ, clear, 0)
+    owner = (lax.axis_index(AX) == 0) & (my_z < OWNERS)
+    numbers = start_loads((tc_ref, tr_ref, lr_ref, slab_ref), (tc, tr, lr, own), num_sem)
+    loads = start_loads(parts_of(blocks_ref), parts_of(buf), in_sem)
     for number in numbers:
         number.wait()
     for i in range(OWNERS):
         pan[i] = jnp.where(owner & (my_z == i), own[...], 0.0)
-    lane = lax.broadcasted_iota(jnp.int32, (NB, TR), 1)
-
-    def add(i, carry):
-        col = tc[0, i]
-        at = pl.ds(pl.multiple_of(tr[0, i] * TR, TR), TR)
-        block = jnp.where(lane < lr[0, i], buf[i], 0.0)
-
+
+    def place(col, at, block):
         @pl.when(col < OWNERS)
         def _():
-            pan[col, :, at] = pan[col, :, at] + block
-
+            pan[col, :, at] = pan[col, :, at] + block()
+
+    add_blocks((tc, tr, lr), loads, buf, place)
+    store = pltpu.make_async_copy(pan, pan_out, out_sem.at[0])
+    store.start()
+    store.wait()
+
+
+def dense_kernel(tc_ref, tr_ref, lr_ref, blocks_ref, *rest):
+    dense_outs = rest[: NZ + 1]
+    tc, tr, lr, buf, dense, in_sem, num_sem, out_sem = rest[NZ + 1 :]
+    my_x = lax.axis_index(AX)
+    my_z = lax.axis_index(AZ)
+    numbers = start_loads((tc_ref, tr_ref, lr_ref), (tc, tr, lr), num_sem)
+    loads = start_loads(parts_of(blocks_ref), parts_of(buf), in_sem)
+
+    def clear(i, carry):
+        dense[i] = jnp.zeros((NB, ROWS_DEV), F32)
+        return carry
+
+    lax.fori_loop(0, NX * NZ, clear, 0)
+    for number in numbers:
+        number.wait()
+
+    def place(col, at, block):
         @pl.when(col >= OWNERS)
         def _():
             slot = ((col % NZ + NZ - my_z) % NZ) * NX + (col // NZ + NX - my_x) % NX
-            dense[slot, :, at] = dense[slot, :, at] + block
-
-        return carry
-
-    for i in range(CB_DEV // CH):
-        loads[i].wait()
-        lax.fori_loop(i * CH, (i + 1) * CH, add, 0)
-    stores = [pltpu.make_async_copy(pan, pan_out, out_sem.at[0])]
-    base = 0
-    for i, out in enumerate(dense_outs):
-        stores.append(pltpu.make_async_copy(dense.at[pl.ds(base, out.shape[0])], out, out_sem.at[1 + i]))
+            dense[slot, :, at] = dense[slot, :, at] + block()
+
+    add_blocks((tc, tr, lr), loads, buf, place)
+    pieces, base = [], 0
+    for out in dense_outs:
+        pieces.append(dense.at[pl.ds(base, out.shape[0])])
         base += out.shape[0]
-    for store in stores:
-        store.start()
+    stores = start_loads(pieces, dense_outs, out_sem)
     for store in stores:
         store.wait()
 
 
 def scatter(tc, tr, lr, blocks, slab):
-    sizes = [NX] * NZ
-    outs = pl.pallas_call(
-        scatter_kernel,
-        out_shape=[jax.ShapeDtypeStruct((n, NB, ROWS_DEV), F32) for n in [OWNERS] + sizes],
+    loads = pltpu.SemaphoreType.DMA((CB_DEV // CH,))
+    numbers = [pltpu.SMEM((1, CB_DEV), jnp.int32)] * 3
+    buf = pltpu.VMEM((CB_DEV, NB, TR), F32)
+    params = pltpu.CompilerParams(vmem_limit_bytes=56 * MIB)
+    pan = pl.pallas_call(
+        panel_kernel,
+        out_shape=jax.ShapeDtypeStruct((OWNERS, NB, ROWS_DEV), F32),
         in_specs=[HBM] * 5,
-        out_specs=[HBM] * (1 + NZ),
-        scratch_shapes=[pltpu.SMEM((1, CB_DEV), jnp.int32)] * 3
-        + [
-            pltpu.VMEM((NB, ROWS_DEV), F32),
-            pltpu.VMEM((CB_DEV, NB, TR), F32),
-            pltpu.VMEM((NX * NZ, NB, ROWS_DEV), F32),
-            pltpu.VMEM((OWNERS, NB, ROWS_DEV), F32),
-            pltpu.SemaphoreType.DMA((CB_DEV // CH,)),
-            pltpu.SemaphoreType.DMA((4,)),
-            pltpu.SemaphoreType.DMA((1 + NZ,)),
-        ],
-        compiler_params=pltpu.CompilerParams(vmem_limit_bytes=56 * MIB),
-        name="scatter",
+        out_specs=HBM,
+        scratch_shapes=numbers
+        + [pltpu.VMEM((NB, ROWS_DEV), F32), buf, pltpu.VMEM((OWNERS, NB, ROWS_DEV), F32), loads]
+        + [pltpu.SemaphoreType.DMA((4,)), pltpu.SemaphoreType.DMA((1,))],
+        compiler_params=params,
+        cost_estimate=pl.CostEstimate(flops=1_000_000, bytes_accessed=3_000_000, transcendentals=0),
+        name="panel_blocks",
     )(tc, tr, lr, blocks, slab)
-    return outs[0], list(outs[1:])
+    dense = pl.pallas_call(
+        dense_kernel,
+        out_shape=[jax.ShapeDtypeStruct((n, NB, ROWS_DEV), F32) for n in [NX] * 4 + [NX // 2] * 2 + [NX] * 3],
+        in_specs=[HBM] * 4,
+        out_specs=[HBM] * (NZ + 1),
+        scratch_shapes=numbers
+        + [buf, pltpu.VMEM((NX * NZ, NB, ROWS_DEV), F32), loads]
+        + [pltpu.SemaphoreType.DMA((3,)), pltpu.SemaphoreType.DMA((NZ + 1,))],
+        compiler_params=params,
+        cost_estimate=pl.CostEstimate(flops=1_000_000, bytes_accessed=40_000_000, transcendentals=0),
+        name="slab_blocks",
+    )(tc, tr, lr, blocks)
+    return pan, list(dense)
 
 
 def shift(value, axis, n, step):
@@ -138,6 +165,20 @@
         else:
             (ahead,) = yield sent
     yield rel[0] + back + ahead
+
+
+def ring_sum_halves(rel, halves, axis, n):
+    h = halves[0].shape[0]
+    ahead, back = yield [shift(halves[0], axis, n, 1), shift(halves[1], axis, n, -1)]
+    for d in range(n // 2 - 1, 0, -1):
+        up, down = rel[d], rel[n - d]
+        if d == n // 2 - 1:
+            up = jnp.concatenate([up[:h] + ahead, up[h:]], axis=0)
+            down = jnp.concatenate([down[:h], down[h:] + back], axis=0)
+        else:
+            up, down = up + ahead, down + back
+        ahead, back = yield [shift(up, axis, n, 1), shift(down, axis, n, -1)]
+    yield rel[0] + ahead + back
 
 
 def tied(value, sent):
@@ -282,7 +323,7 @@
     pick = (pivot[:, None] == row_group * ROWS_DEV + jnp.arange(ROWS_DEV)[None, :]).astype(F32)
     hit = jnp.sum(pick, axis=0) > 0
 
-    along_z = ring_sum(dense, AZ, NZ)
+    along_z = ring_sum_halves(dense[:4] + [None] + dense[6:], dense[4:6], AZ, NZ)
     pair = next(along_z)
     chunk = exchange(pan, AX).sum(axis=0).reshape(NZ, NB // NZ, ROWS_DEV)
     chunk, pair = tied(chunk, pair)

time: 120 us -> 119 us (level)
  starting transfers between devices: 48.9 us -> 46.2 us
  Pallas kernels: 22.4 us -> 24.4 us
  waiting for transfers between devices: 24.9 us -> 23.2 us
  other arithmetic: 3.09 us -> 4.65 us
    all_to_all x5, waiting for transfers between devices: 11.5 us -> 8.31 us  [exchange(): return lax.all_to_all(value, axis, split_axis=0, concat_axis=0, tiled=True)]
    all_to_all x5, starting transfers between devices: 34.5 us -> 31.4 us  [exchange(): return lax.all_to_all(value, axis, split_axis=0, concat_axis=0, tiled=True)]
    pallas_call x1 -> x2, Pallas kernels: 4.88 us -> 6.84 us  [the longest x1 4.04 us: scatter(): pl.pallas_call(dense_kernel, out_shape=[jax.ShapeDtypeStruct((n, NB, ROWS...]
    add x3 -> x6, other arithmetic: 1.11 us -> 2.84 us  [the longest x1 1.33 us: ring_sum_halves(): up = jnp.concatenate([up[:h] + ahead, up[h:]], axis=0)]
    ppermute x10 -> x11, waiting for transfers between devices: 13.4 us -> 14.8 us  [shift(): return lax.ppermute(value, axis, [(i, (i + step) % n) for i in range(n)])]
    ppermute x10 -> x11, starting transfers between devices: 14.3 us -> 14.9 us  [shift(): return lax.ppermute(value, axis, [(i, (i + step) % n) for i in range(n)])]
  transfers between devices with their start and end apart: 15 -> 16, of which waited for: 7 -> 6; matrix products, arithmetic and copies ran while one was open for 5% -> 6% of each run, Pallas kernels for 13% -> 16%
where the time goes in v3:
time: 119 us; the launch traced here: 118 us
  starting transfers between devices  46.2 us (39%)
  Pallas kernels  24.4 us (21%)
  waiting for transfers between devices  23.2 us (19%)
  blocking collectives  15.5 us (13%)
  other arithmetic  4.65 us (4%)
  local copies, waits for them, and re-layouts  3.02 us (3%)
    all_to_all x5, starting transfers between devices, exchange(): return lax.all_to_all(value, axis, split_axis=0, concat_axis=0, tiled=True)  31.4 us
    all_to_all x1, blocking collectives, exchange(): return lax.all_to_all(value, axis, split_axis=0, concat_axis=0, tiled=True)  15.5 us
    pallas_call x1, Pallas kernels, factor(): pl.pallas_call(factor_kernel, out_shape=[jax.ShapeDtypeStruct((PW, PW), F...  15.4 us
    ppermute x11, starting transfers between devices, shift(): return lax.ppermute(value, axis, [(i, (i + step) % n) for i in range(n)])  14.9 us
    ppermute x11, waiting for transfers between devices, shift(): return lax.ppermute(value, axis, [(i, (i + step) % n) for i in range(n)])  14.8 us
    all_to_all x5, waiting for transfers between devices, exchange(): return lax.all_to_all(value, axis, split_axis=0, concat_axis=0, tiled=True)  8.31 us
    pallas_call x1, Pallas kernels, scatter(): pl.pallas_call(dense_kernel, out_shape=[jax.ShapeDtypeStruct((n, NB, ROWS...  4.04 us
    pallas_call x1, Pallas kernels, scatter(): pl.pallas_call(panel_kernel, out_shape=jax.ShapeDtypeStruct((OWNERS, NB,...  2.8 us
  transfers between devices with their start and end apart: 16, of which 6 were waited for; matrix products, arithmetic and copies ran while one was open for 6% of the time, Pallas kernels for 16%

profile of v3, /device:TPU:1, one launch (start us, length us, event | category | flops | bytes accessed | tf_op | source)
XLA Modules:
  0.0 118.4 jit_solution(17988851115049699503)
XLA Ops:
  0.0 2.8 %panel_blocks.1 = f32[4,64,512]{2,1,0:T(8,128)} custom-call(s32[1,32]{1,0:T(1,128)} %tc_ref.3, s32[1,32]{1,0:T(1,128)} %tr_ref.3, s32[1,32]{1,0:T(1,128)} %lr_ref.3, f32[32,64,256]{2,1,0:T(8,128)} %bitcast.27, f32[64,512]{1,0:T(8,128)} %slab_ref.1), custom_call_target="tpu_custom_call" | custom-call | flops 1000000 | bytes 3000000 | tf_op jit(solution)/shard_map/panel_blocks/pallas_call | solution.py:127
  2.8 4.8 %all-to-all-start = ((f32[4,64,512]{2,1,0:T(8,128)}), f32[4,64,512]{2,1,0:T(8,128)S(1)}, u32[]{:S(2)}, u32[]{:S(2)}) async-start(f32[4,64,512]{2,1,0:T(8,128)} %panel_blocks.1), calls=%async_computation | async-start | bytes 1048576 | tf_op jit(solution)/shard_map/all_to_all | solution.py:189
  7.7 4.0 %slab_blocks.1 = (f32[4,64,512]{2,1,0:T(8,128)}, f32[4,64,512]{2,1,0:T(8,128)}, f32[4,64,512]{2,1,0:T(8,128)}, f32[4,64,512]{2,1,0:T(8,128)}, f32[2,64,512]{2,1,...) custom-call(s32[1,32]{1,0:T(1,128)} %tc_ref.3, ...), custom_call_target="tpu_custom_call" | custom-call | flops 1000000 | bytes 40000000 | tf_op jit(solution)/shard_map/slab_blocks/pallas_call | solution.py:139
  11.7 1.8 %collective-permute-start = (f32[2,64,512]{2,1,0:T(8,128)}, f32[2,64,512]{2,1,0:T(8,128)S(1)}, u32[]{:S(2)}, u32[]{:S(2)}) collective-permute-start(f32[2,64,512]{2,1,0:T(8,128)} %get-tuple-element.32), channel_id=1, source_target_pairs={{0,1},{1,2},{2,3},{3,4},{4,5},{5,6},{6,7},{7,0},{8,9},{9,10},{10,1... | collective-permute-start | bytes 786440 | tf_op jit(solution)/shard_map/ppermute | solution.py:155
  13.5 4.0 %collective-permute-start.1 = (f32[2,64,512]{2,1,0:T(8,128)}, f32[2,64,512]{2,1,0:T(8,128)S(1)}, u32[]{:S(2)}, u32[]{:S(2)}) collective-permute-start(f32[2,64,512]{2,1,0:T(8,128)} %get-tuple-element.33), channel_id=1, source_target_pairs={{0,7},{1,0},{2,1},{3,2},{4,3},{5,4},{6,5},{7,6},{8,15},{9,8},{10,9... | collective-permute-start | bytes 786440 | tf_op jit(solution)/shard_map/ppermute | solution.py:155
  17.7 0.7 reduce_sum.36
  18.4 6.5 %all-to-all-start.1 = ((f32[8,8,512]{2,1,0:T(8,128)}), f32[8,8,512]{2,1,0:T(8,128)S(1)}, u32[]{:S(2)}, u32[]{:S(2)}) async-start(f32[8,8,512]{2,1,0:T(8,128)} %bitcast.2), calls=%async_computation.1 | async-start | bytes 262144 | tf_op jit(solution)/shard_map/all_to_all | solution.py:189
  24.8 1.3 %slice_add_fusion.1 = (f32[2,64,512]{2,1,0:T(8,128)S(1)}, f32[2,64,512]{2,1,0:T(8,128)S(1)}, f32[2,64,512]{2,1,0:T(8,128)S(1)}, f32[2,64,512]{2,1,0:T(8,128)S(1)}) fusion(f32[2,64,512]{2,1,0:T(8,128)S(1)} %collective-permute-done, f32[4,64,512]{2,1,0:T(8,128)} %get-tuple-element.31, f32[2,64,512]{2,1,0:T(8,128)S(1)} %collective-permute-done.1, ...), kind=kLoop, calls=%fused_computation.12 | loop fusion | flops 131072 | bytes 2621440 | tf_op jit(solution)/shard_map/add | solution.py:176
  26.3 2.7 %collective-permute-start.3 = (f32[4,64,512]{2,1,0:T(8,128)S(1)}, f32[4,64,512]{2,1,0:T(8,128)S(1)}, u32[]{:S(2)}, u32[]{:S(2)}) collective-permute-start(f32[4,64,512]{2,1,0:T(8,128)S(1)} %pad_maximum_fusion.1), channel_id=1, source_target_pairs={{0,7},{1,0},{2,1},{3,2},{4,3},{5,4},{6,5},{7,6},{8,15},{9,8},{10,9... | collective-permute-start | bytes 1572872 | tf_op jit(solution)/shard_map/ppermute | solution.py:155
  29.0 0.8 pad_maximum_fusion
  29.8 3.0 %all-to-all-done.1 = f32[8,8,512]{2,1,0:T(8,128)S(1)} async-done(((f32[8,8,512]{2,1,0:T(8,128)}), f32[8,8,512]{2,1,0:T(8,128)S(1)}, u32[]{:S(2)}, u32[]{:S(2)}) %all-to-all-start.1) | async-done | bytes 131104 | tf_op jit(solution)/shard_map/all_to_all | solution.py:189
  33.3 0.7 broadcast_in_dim.22
  34.0 8.3 %all-to-all-start.2 = ((f32[8,8,512]{2,1,0:T(8,128)}), f32[8,8,512]{2,1,0:T(8,128)S(1)}, u32[]{:S(2)}, u32[]{:S(2)}) async-start(f32[8,8,512]{2,1,0:T(8,128)} %broadcast_in_dim.22), calls=%async_computation.2 | async-start | bytes 262144 | tf_op jit(solution)/shard_map/all_to_all | solution.py:189
  42.3 5.3 %all-to-all-done.2 = f32[8,8,512]{2,1,0:T(8,128)S(1)} async-done(((f32[8,8,512]{2,1,0:T(8,128)}), f32[8,8,512]{2,1,0:T(8,128)S(1)}, u32[]{:S(2)}, u32[]{:S(2)}) %all-to-all-start.2) | async-done | bytes 131104 | tf_op jit(solution)/shard_map/all_to_all | solution.py:189
  48.0 0.4 collective-permute-start.5
  48.5 1.2 collective-permute-start.4
  49.7 15.5 %all_to_all.30 = f32[8,8,768]{2,1,0:T(8,128)S(1)} all-to-all(f32[8,8,768]{2,1,0:T(8,128)S(1)} %broadcast_in_dim.24), channel_id=1, replica_groups=mesh['prow'=8,'pcol_0'=4,'pcol_1'=8] {'pcol_1'}, dimensions={0} | all-to-all | bytes 393216 | tf_op jit(solution)/shard_map/all_to_all | solution.py:189
  65.4 0.5 collective-permute-start.7
  66.0 1.1 collective-permute-start.6
  67.1 0.9 broadcast_in_dim.25
  68.0 3.6 %all-to-all-start.4 = ((f32[4,64,768]{2,1,0:T(8,128)}), f32[4,64,768]{2,1,0:T(8,128)S(1)}, u32[]{:S(2)}, u32[]{:S(2)}) async-start(f32[4,64,768]{2,1,0:T(8,128)} %broadcast_in_dim.25), calls=%async_computation.4 | async-start | bytes 1572864 | tf_op jit(solution)/shard_map/all_to_all | solution.py:189
  71.6 4.2 %collective-permute-done.7 = f32[4,64,512]{2,1,0:T(8,128)S(1)} collective-permute-done((f32[4,64,512]{2,1,0:T(8,128)S(1)}, f32[4,64,512]{2,1,0:T(8,128)S(1)}, u32[]{:S(2)}, u32[]{:S(2)}) %collective-permute-start.7) | collective-permute-done | bytes 524320 | tf_op jit(solution)/shard_map/ppermute | solution.py:155
  75.8 1.5 %collective-permute-done.6 = f32[4,64,512]{2,1,0:T(8,128)} collective-permute-done((f32[4,64,512]{2,1,0:T(8,128)S(1)}, f32[4,64,512]{2,1,0:T(8,128)}, u32[]{:S(2)}, u32[]{:S(2)}) %collective-permute-start.6) | collective-permute-done | bytes 524320 | tf_op jit(solution)/shard_map/ppermute | solution.py:155
  77.3 1.2 %add_add_fusion = f32[4,64,512]{2,1,0:T(8,128)S(1)} fusion(f32[4,64,512]{2,1,0:T(8,128)S(1)} %collective-permute-done.7, f32[4,64,512]{2,1,0:T(8,128)S(1)} %copy-done.5, f32[4,64,512]{2,1,0:T(8,128)} %collective-permute-done.6), kind=kLoop, calls=%fused_computation.10 | loop fusion | flops 262144 | bytes 2097152 | tf_op jit(solution)/shard_map/add | solution.py:181
  78.9 2.4 %collective-permute-start.9 = (f32[64,512]{1,0:T(8,128)S(1)}, f32[64,512]{1,0:T(8,128)S(1)}, u32[]{:S(2)}, u32[]{:S(2)}) collective-permute-start(f32[64,512]{1,0:T(8,128)S(1)} %get-tuple-element.51), channel_id=1, source_target_pairs={{0,24},{8,0},{16,8},{24,16},{1,25},{9,1},{17,9},{25,17},{2,26},{10... | collective-permute-start | bytes 393224 | tf_op jit(solution)/shard_map/ppermute | solution.py:155
  81.3 4.3 %collective-permute-done.8 = f32[64,512]{1,0:T(8,128)S(1)} collective-permute-done((f32[64,512]{1,0:T(8,128)S(1)}, f32[64,512]{1,0:T(8,128)S(1)}, u32[]{:S(2)}, u32[]{:S(2)}) %collective-permute-start.8) | collective-permute-done | bytes 131104 | tf_op jit(solution)/shard_map/ppermute | solution.py:155
  85.9 4.8 %collective-permute-done.10 = f32[64,512]{1,0:T(8,128)S(1)} collective-permute-done((f32[64,512]{1,0:T(8,128)S(1)}, f32[64,512]{1,0:T(8,128)S(1)}, u32[]{:S(2)}, u32[]{:S(2)}) %collective-permute-start.10) | collective-permute-done | bytes 131104 | tf_op jit(solution)/shard_map/ppermute | solution.py:155
  90.8 0.4 fusion
  91.3 1.1 broadcast_in_dim.26
  92.4 8.2 %all-to-all-start.5 = ((f32[8,64,512]{2,1,0:T(8,128)}), f32[8,64,512]{2,1,0:T(8,128)S(1)}, u32[]{:S(2)}, u32[]{:S(2)}) async-start(f32[8,64,512]{2,1,0:T(8,128)} %broadcast_in_dim.26), calls=%async_computation.5 | async-start | bytes 2097152 | tf_op jit(solution)/shard_map/slab_swap/all_to_all | solution.py:189
  100.8 15.4 %factor.1 = (f32[256,256]{1,0:T(8,128)S(1)}, f32[256,256]{1,0:T(8,128)S(1)}, f32[256,256]{1,0:T(8,128)S(1)}) custom-call(f32[256,256]{1,0:T(8,128)S(1)} %slice.65.t_ref), custom_call_target="tpu_custom_call" | custom-call | flops 40000000 | bytes 60000000 | tf_op jit(solution)/shard_map/factor/pallas_call | solution.py:267
  116.2 2.1 %finish.1 = f32[64,512]{1,0:T(8,128)} custom-call(s32[256,1]{1,0:T(8,128)S(1)} %copy.8.pivot_ref, f32[64,512]{1,0:T(8,128)S(1)} %fusion.15.matrix_ref, f32[8,64,512]{2,1,0:T(8,128)S(1)} %all-to-all-done.5.offers_ref, f32[256,512]{1,0:T(8,128)S(1)} %slice.64.panel_ref, f32[256,256]{1,0:T(8,128)S(1)} %get-tuple-element.48.packed_ref, ...), custom_call_target="tpu_custom_call" | custom-call | tf_op jit(solution)/shard_map/finish/pallas_call | solution.py:308
  (51 shorter events, 2.3 us)
Async XLA Ops:
  2.8 14.7 %copy-start.6 = (s32[1,256]{1,0:T(1,128)S(1)}, s32[1,256]{1,0:T(1,128)}, u32[]{:S(2)}) copy-start(s32[1,256]{1,0:T(1,128)} %param.11) | copy-start | bytes 3076
  2.8 14.8 %all-to-all-start = ((f32[4,64,512]{2,1,0:T(8,128)}), f32[4,64,512]{2,1,0:T(8,128)S(1)}, u32[]{:S(2)}, u32[]{:S(2)}) async-start(f32[4,64,512]{2,1,0:T(8,128)} %panel_blocks.1), calls=%async_computation | async-start | bytes 1048576 | tf_op jit(solution)/shard_map/all_to_all | solution.py:189
  11.7 13.1 %collective-permute-start = (f32[2,64,512]{2,1,0:T(8,128)}, f32[2,64,512]{2,1,0:T(8,128)S(1)}, u32[]{:S(2)}, u32[]{:S(2)}) collective-permute-start(f32[2,64,512]{2,1,0:T(8,128)} %get-tuple-element.32), channel_id=1, source_target_pairs={{0,1},{1,2},{2,3},{3,4},{4,5},{5,6},{6,7},{7,0},{8,9},{9,10},{10,1... | collective-permute-start | bytes 786440 | tf_op jit(solution)/shard_map/ppermute | solution.py:155
  13.5 11.3 %collective-permute-start.1 = (f32[2,64,512]{2,1,0:T(8,128)}, f32[2,64,512]{2,1,0:T(8,128)S(1)}, u32[]{:S(2)}, u32[]{:S(2)}) collective-permute-start(f32[2,64,512]{2,1,0:T(8,128)} %get-tuple-element.33), channel_id=1, source_target_pairs={{0,7},{1,0},{2,1},{3,2},{4,3},{5,4},{6,5},{7,6},{8,15},{9,8},{10,9... | collective-permute-start | bytes 786440 | tf_op jit(solution)/shard_map/ppermute | solution.py:155
  18.4 14.5 %all-to-all-start.1 = ((f32[8,8,512]{2,1,0:T(8,128)}), f32[8,8,512]{2,1,0:T(8,128)S(1)}, u32[]{:S(2)}, u32[]{:S(2)}) async-start(f32[8,8,512]{2,1,0:T(8,128)} %bitcast.2), calls=%async_computation.1 | async-start | bytes 262144 | tf_op jit(solution)/shard_map/all_to_all | solution.py:189
  26.2 21.7 %copy-start.3 = (f32[4,64,512]{2,1,0:T(8,128)S(1)}, f32[4,64,512]{2,1,0:T(8,128)}, u32[]{:S(2)}) copy-start(f32[4,64,512]{2,1,0:T(8,128)} %get-tuple-element.38) | copy-start | bytes 1572868
  26.2 22.2 %copy-start.2 = (f32[4,64,512]{2,1,0:T(8,128)S(1)}, f32[4,64,512]{2,1,0:T(8,128)}, u32[]{:S(2)}) copy-start(f32[4,64,512]{2,1,0:T(8,128)} %get-tuple-element.30) | copy-start | bytes 1572868
  26.3 21.6 %collective-permute-start.3 = (f32[4,64,512]{2,1,0:T(8,128)S(1)}, f32[4,64,512]{2,1,0:T(8,128)S(1)}, u32[]{:S(2)}, u32[]{:S(2)}) collective-permute-start(f32[4,64,512]{2,1,0:T(8,128)S(1)} %pad_maximum_fusion.1), channel_id=1, source_target_pairs={{0,7},{1,0},{2,1},{3,2},{4,3},{5,4},{6,5},{7,6},{8,15},{9,8},{10,9... | collective-permute-start | bytes 1572872 | tf_op jit(solution)/shard_map/ppermute | solution.py:155
  29.8 18.0 %collective-permute-start.2 = (f32[4,64,512]{2,1,0:T(8,128)}, f32[4,64,512]{2,1,0:T(8,128)S(1)}, u32[]{:S(2)}, u32[]{:S(2)}) collective-permute-start(f32[4,64,512]{2,1,0:T(8,128)} %pad_maximum_fusion), channel_id=1, source_target_pairs={{0,1},{1,2},{2,3},{3,4},{4,5},{5,6},{6,7},{7,0},{8,9},{9,10},{10,1... | collective-permute-start | bytes 1572872 | tf_op jit(solution)/shard_map/ppermute | solution.py:155
  34.0 31.3 %copy-start.1 = (f32[4,64,512]{2,1,0:T(8,128)S(1)}, f32[4,64,512]{2,1,0:T(8,128)}, u32[]{:S(2)}) copy-start(f32[4,64,512]{2,1,0:T(8,128)} %get-tuple-element.41) | copy-start | bytes 1572868
  34.0 13.6 %all-to-all-start.2 = ((f32[8,8,512]{2,1,0:T(8,128)}), f32[8,8,512]{2,1,0:T(8,128)S(1)}, u32[]{:S(2)}, u32[]{:S(2)}) async-start(f32[8,8,512]{2,1,0:T(8,128)} %broadcast_in_dim.22), calls=%async_computation.2 | async-start | bytes 262144 | tf_op jit(solution)/shard_map/all_to_all | solution.py:189
  48.0 17.9 %copy-start = (f32[4,64,512]{2,1,0:T(8,128)S(1)}, f32[4,64,512]{2,1,0:T(8,128)}, u32[]{:S(2)}) copy-start(f32[4,64,512]{2,1,0:T(8,128)} %get-tuple-element.29) | copy-start | bytes 1572868
  48.0 17.3 %collective-permute-start.5 = (f32[4,64,512]{2,1,0:T(8,128)S(1)}, f32[4,64,512]{2,1,0:T(8,128)S(1)}, u32[]{:S(2)}, u32[]{:S(2)}) collective-permute-start(f32[4,64,512]{2,1,0:T(8,128)S(1)} %add.52), channel_id=1, source_target_pairs={{0,7},{1,0},{2,1},{3,2},{4,3},{5,4},{6,5},{7,6},{8,15},{9,8},{10,9... | collective-permute-start | bytes 1572872 | tf_op jit(solution)/shard_map/ppermute | solution.py:155
  48.5 16.7 %collective-permute-start.4 = (f32[4,64,512]{2,1,0:T(8,128)S(1)}, f32[4,64,512]{2,1,0:T(8,128)S(1)}, u32[]{:S(2)}, u32[]{:S(2)}) collective-permute-start(f32[4,64,512]{2,1,0:T(8,128)S(1)} %add.51), channel_id=1, source_target_pairs={{0,1},{1,2},{2,3},{3,4},{4,5},{5,6},{6,7},{7,0},{8,9},{9,10},{10,1... | collective-permute-start | bytes 1572872 | tf_op jit(solution)/shard_map/ppermute | solution.py:155
  65.3 12.0 %copy-start.5 = (f32[4,64,512]{2,1,0:T(8,128)S(1)}, f32[4,64,512]{2,1,0:T(8,128)}, u32[]{:S(2)}) copy-start(f32[4,64,512]{2,1,0:T(8,128)} %get-tuple-element.28) | copy-start | bytes 1572868
  65.4 10.5 %collective-permute-start.7 = (f32[4,64,512]{2,1,0:T(8,128)S(1)}, f32[4,64,512]{2,1,0:T(8,128)S(1)}, u32[]{:S(2)}, u32[]{:S(2)}) collective-permute-start(f32[4,64,512]{2,1,0:T(8,128)S(1)} %add.54), channel_id=1, source_target_pairs={{0,7},{1,0},{2,1},{3,2},{4,3},{5,4},{6,5},{7,6},{8,15},{9,8},{10,9... | collective-permute-start | bytes 1572872 | tf_op jit(solution)/shard_map/ppermute | solution.py:155
  66.0 11.3 %collective-permute-start.6 = (f32[4,64,512]{2,1,0:T(8,128)S(1)}, f32[4,64,512]{2,1,0:T(8,128)}, u32[]{:S(2)}, u32[]{:S(2)}) collective-permute-start(f32[4,64,512]{2,1,0:T(8,128)S(1)} %add.53), channel_id=1, source_target_pairs={{0,1},{1,2},{2,3},{3,4},{4,5},{5,6},{6,7},{7,0},{8,9},{9,10},{10,1... | collective-permute-start | bytes 1572872 | tf_op jit(solution)/shard_map/ppermute | solution.py:155
  68.0 22.8 %copy-start.4 = (f32[64,512]{1,0:T(8,128)S(1)}, f32[64,512]{1,0:T(8,128)}, u32[]{:S(2)}) copy-start(f32[64,512]{1,0:T(8,128)} %slab_ref.1) | copy-start | bytes 393220
  68.0 13.3 %all-to-all-start.4 = ((f32[4,64,768]{2,1,0:T(8,128)}), f32[4,64,768]{2,1,0:T(8,128)S(1)}, u32[]{:S(2)}, u32[]{:S(2)}) async-start(f32[4,64,768]{2,1,0:T(8,128)} %broadcast_in_dim.25), calls=%async_computation.4 | async-start | bytes 1572864 | tf_op jit(solution)/shard_map/all_to_all | solution.py:189
  78.5 7.1 %collective-permute-start.8 = (f32[64,512]{1,0:T(8,128)S(1)}, f32[64,512]{1,0:T(8,128)S(1)}, u32[]{:S(2)}, u32[]{:S(2)}) collective-permute-start(f32[64,512]{1,0:T(8,128)S(1)} %get-tuple-element.52), channel_id=1, source_target_pairs={{0,8},{8,16},{16,24},{24,0},{1,9},{9,17},{17,25},{25,1},{2,10},{10... | collective-permute-start | bytes 393224 | tf_op jit(solution)/shard_map/ppermute | solution.py:155
  78.9 6.7 %collective-permute-start.9 = (f32[64,512]{1,0:T(8,128)S(1)}, f32[64,512]{1,0:T(8,128)S(1)}, u32[]{:S(2)}, u32[]{:S(2)}) collective-permute-start(f32[64,512]{1,0:T(8,128)S(1)} %get-tuple-element.51), channel_id=1, source_target_pairs={{0,24},{8,0},{16,8},{24,16},{1,25},{9,1},{17,9},{25,17},{2,26},{10... | collective-permute-start | bytes 393224 | tf_op jit(solution)/shard_map/ppermute | solution.py:155
  85.7 5.1 %collective-permute-start.10 = (f32[64,512]{1,0:T(8,128)S(1)}, f32[64,512]{1,0:T(8,128)S(1)}, u32[]{:S(2)}, u32[]{:S(2)}) collective-permute-start(f32[64,512]{1,0:T(8,128)S(1)} %fusion.12), channel_id=1, source_target_pairs={{0,8},{8,16},{16,24},{24,0},{1,9},{9,17},{17,25},{25,1},{2,10},{10... | collective-permute-start | bytes 393224 | tf_op jit(solution)/shard_map/ppermute | solution.py:155
  92.4 23.8 %all-to-all-start.5 = ((f32[8,64,512]{2,1,0:T(8,128)}), f32[8,64,512]{2,1,0:T(8,128)S(1)}, u32[]{:S(2)}, u32[]{:S(2)}) async-start(f32[8,64,512]{2,1,0:T(8,128)} %broadcast_in_dim.26), calls=%async_computation.5 | async-start | bytes 2097152 | tf_op jit(solution)/shard_map/slab_swap/all_to_all | solution.py:189

commit v4 on v3

--- a/solution.py
+++ b/solution.py
@@ -276,6 +276,25 @@
     )(t)
 
 
+def offer_kernel(matrix_ref, pick_ref, out_ref):
+    matrix = matrix_ref[...]
+    offer = dot_nt(matrix, pick_ref[...])
+    for i in range(PROW):
+        out_ref[i, :, :PW] = offer
+        out_ref[i, :, PW:] = matrix[:, :PW]
+
+
+def offered(matrix, pick):
+    return pl.pallas_call(
+        offer_kernel,
+        out_shape=jax.ShapeDtypeStruct((PROW, NB, 2 * PW), F32),
+        in_specs=[VMEM] * 2,
+        out_specs=VMEM,
+        compiler_params=pltpu.CompilerParams(vmem_limit_bytes=16 * MIB),
+        name="offer",
+    )(matrix, pick)
+
+
 def finish_kernel(pivot_ref, matrix_ref, offers_ref, panel_ref, packed_ref, loinv_ref, upinv_ref, out_ref, low_ref):
     row_group = lax.axis_index(AY)
     col_group = lax.axis_index(AX) * NZ + lax.axis_index(AZ)
@@ -346,9 +365,9 @@
     pair = along_x.send(pair)
     matrix = matrix_slab + along_x.send(pair)
     with jax.named_scope("slab_swap"):
-        offer = jnp.concatenate([dot_nt(matrix, pick), matrix[:, :PW]], axis=1)
+        offer = offered(matrix, pick)
         diag = lax.optimization_barrier((both[:, :PW], offer))[0]
-        offers = gather(offer, AY, PROW)
+        offers = exchange(offer, AY)
     packed, loinv, upinv = factor(diag)
     return finish(pivot[:, None], matrix, offers, both[:, PW:], packed, loinv, upinv)
 

time: 119 us -> 119 us (level)
  Pallas kernels: 24.4 us -> 26 us
    pallas_call x0 -> x1, Pallas kernels: none -> 1.65 us  [offered(): pl.pallas_call(offer_kernel, out_shape=jax.ShapeDtypeStruct((PROW, NB, 2...]
    broadcast_in_dim x4 -> x3, local copies, waits for them, and re-layouts: 2.75 us -> 1.62 us  [copied(): return jnp.broadcast_to(value, (n, *value.shape))]
where the time goes in v4:
time: 119 us; the launch traced here: 118 us
  starting transfers between devices  45.9 us (39%)
  Pallas kernels  26 us (22%)
  waiting for transfers between devices  23.3 us (20%)
  blocking collectives  15.5 us (13%)
  other arithmetic  4.73 us (4%)
  local copies, waits for them, and re-layouts  1.89 us (2%)
    all_to_all x5, starting transfers between devices, exchange(): return lax.all_to_all(value, axis, split_axis=0, concat_axis=0, tiled=True)  31.3 us
    all_to_all x1, blocking collectives, exchange(): return lax.all_to_all(value, axis, split_axis=0, concat_axis=0, tiled=True)  15.5 us
    pallas_call x1, Pallas kernels, factor(): pl.pallas_call(factor_kernel, out_shape=[jax.ShapeDtypeStruct((PW, PW), F...  15.4 us
    ppermute x11, waiting for transfers between devices, shift(): return lax.ppermute(value, axis, [(i, (i + step) % n) for i in range(n)])  14.9 us
    ppermute x11, starting transfers between devices, shift(): return lax.ppermute(value, axis, [(i, (i + step) % n) for i in range(n)])  14.7 us
    all_to_all x5, waiting for transfers between devices, exchange(): return lax.all_to_all(value, axis, split_axis=0, concat_axis=0, tiled=True)  8.31 us
    pallas_call x1, Pallas kernels, scatter(): pl.pallas_call(dense_kernel, out_shape=[jax.ShapeDtypeStruct((n, NB, ROWS...  4.1 us
    pallas_call x1, Pallas kernels, scatter(): pl.pallas_call(panel_kernel, out_shape=jax.ShapeDtypeStruct((OWNERS, NB,...  2.78 us
  transfers between devices with their start and end apart: 16, of which 6 were waited for; matrix products, arithmetic and copies ran while one was open for 6% of the time, Pallas kernels for 16%

profile of v4, /device:TPU:1, one launch (start us, length us, event | category | flops | bytes accessed | tf_op | source)
XLA Modules:
  0.0 118.4 jit_solution(10436594572188730895)
XLA Ops:
  0.0 2.8 %panel_blocks.1 = f32[4,64,512]{2,1,0:T(8,128)} custom-call(s32[1,32]{1,0:T(1,128)} %tc_ref.3, s32[1,32]{1,0:T(1,128)} %tr_ref.3, s32[1,32]{1,0:T(1,128)} %lr_ref.3, f32[32,64,256]{2,1,0:T(8,128)} %bitcast.26, f32[64,512]{1,0:T(8,128)} %slab_ref.1), custom_call_target="tpu_custom_call" | custom-call | flops 1000000 | bytes 3000000 | tf_op jit(solution)/shard_map/panel_blocks/pallas_call | solution.py:127
  2.8 4.9 %all-to-all-start = ((f32[4,64,512]{2,1,0:T(8,128)}), f32[4,64,512]{2,1,0:T(8,128)S(1)}, u32[]{:S(2)}, u32[]{:S(2)}) async-start(f32[4,64,512]{2,1,0:T(8,128)} %panel_blocks.1), calls=%async_computation | async-start | bytes 1048576 | tf_op jit(solution)/shard_map/all_to_all | solution.py:189
  7.7 4.1 %slab_blocks.1 = (f32[4,64,512]{2,1,0:T(8,128)}, f32[4,64,512]{2,1,0:T(8,128)}, f32[4,64,512]{2,1,0:T(8,128)}, f32[4,64,512]{2,1,0:T(8,128)}, f32[2,64,512]{2,1,...) custom-call(s32[1,32]{1,0:T(1,128)} %tc_ref.3, ...), custom_call_target="tpu_custom_call" | custom-call | flops 1000000 | bytes 40000000 | tf_op jit(solution)/shard_map/slab_blocks/pallas_call | solution.py:139
  11.8 1.7 %collective-permute-start = (f32[2,64,512]{2,1,0:T(8,128)}, f32[2,64,512]{2,1,0:T(8,128)S(1)}, u32[]{:S(2)}, u32[]{:S(2)}) collective-permute-start(f32[2,64,512]{2,1,0:T(8,128)} %get-tuple-element.32), channel_id=1, source_target_pairs={{0,1},{1,2},{2,3},{3,4},{4,5},{5,6},{6,7},{7,0},{8,9},{9,10},{10,1... | collective-permute-start | bytes 786440 | tf_op jit(solution)/shard_map/ppermute | solution.py:155
  13.4 4.1 %collective-permute-start.1 = (f32[2,64,512]{2,1,0:T(8,128)}, f32[2,64,512]{2,1,0:T(8,128)S(1)}, u32[]{:S(2)}, u32[]{:S(2)}) collective-permute-start(f32[2,64,512]{2,1,0:T(8,128)} %get-tuple-element.33), channel_id=1, source_target_pairs={{0,7},{1,0},{2,1},{3,2},{4,3},{5,4},{6,5},{7,6},{8,15},{9,8},{10,9... | collective-permute-start | bytes 786440 | tf_op jit(solution)/shard_map/ppermute | solution.py:155
  17.6 0.7 reduce_sum.36
  18.3 6.5 %all-to-all-start.1 = ((f32[8,8,512]{2,1,0:T(8,128)}), f32[8,8,512]{2,1,0:T(8,128)S(1)}, u32[]{:S(2)}, u32[]{:S(2)}) async-start(f32[8,8,512]{2,1,0:T(8,128)} %bitcast.2), calls=%async_computation.1 | async-start | bytes 262144 | tf_op jit(solution)/shard_map/all_to_all | solution.py:189
  24.9 1.3 %slice_add_fusion.1 = (f32[2,64,512]{2,1,0:T(8,128)S(1)}, f32[2,64,512]{2,1,0:T(8,128)S(1)}, f32[2,64,512]{2,1,0:T(8,128)S(1)}, f32[2,64,512]{2,1,0:T(8,128)S(1)}) fusion(f32[2,64,512]{2,1,0:T(8,128)S(1)} %collective-permute-done, f32[4,64,512]{2,1,0:T(8,128)} %get-tuple-element.31, f32[2,64,512]{2,1,0:T(8,128)S(1)} %collective-permute-done.1, ...), kind=kLoop, calls=%fused_computation.9 | loop fusion | flops 131072 | bytes 2621440 | tf_op jit(solution)/shard_map/add | solution.py:176
  26.3 2.7 %collective-permute-start.3 = (f32[4,64,512]{2,1,0:T(8,128)S(1)}, f32[4,64,512]{2,1,0:T(8,128)S(1)}, u32[]{:S(2)}, u32[]{:S(2)}) collective-permute-start(f32[4,64,512]{2,1,0:T(8,128)S(1)} %pad_maximum_fusion.1), channel_id=1, source_target_pairs={{0,7},{1,0},{2,1},{3,2},{4,3},{5,4},{6,5},{7,6},{8,15},{9,8},{10,9... | collective-permute-start | bytes 1572872 | tf_op jit(solution)/shard_map/ppermute | solution.py:155
  29.0 0.8 pad_maximum_fusion
  29.8 3.0 %all-to-all-done.1 = f32[8,8,512]{2,1,0:T(8,128)S(1)} async-done(((f32[8,8,512]{2,1,0:T(8,128)}), f32[8,8,512]{2,1,0:T(8,128)S(1)}, u32[]{:S(2)}, u32[]{:S(2)}) %all-to-all-start.1) | async-done | bytes 131104 | tf_op jit(solution)/shard_map/all_to_all | solution.py:189
  32.9 0.4 fusion.1
  33.3 0.7 broadcast_in_dim.19
  34.0 8.3 %all-to-all-start.2 = ((f32[8,8,512]{2,1,0:T(8,128)}), f32[8,8,512]{2,1,0:T(8,128)S(1)}, u32[]{:S(2)}, u32[]{:S(2)}) async-start(f32[8,8,512]{2,1,0:T(8,128)} %broadcast_in_dim.19), calls=%async_computation.2 | async-start | bytes 262144 | tf_op jit(solution)/shard_map/all_to_all | solution.py:189
  42.2 5.3 %all-to-all-done.2 = f32[8,8,512]{2,1,0:T(8,128)S(1)} async-done(((f32[8,8,512]{2,1,0:T(8,128)}), f32[8,8,512]{2,1,0:T(8,128)S(1)}, u32[]{:S(2)}, u32[]{:S(2)}) %all-to-all-start.2) | async-done | bytes 131104 | tf_op jit(solution)/shard_map/all_to_all | solution.py:189
  48.0 0.5 collective-permute-start.5
  48.5 1.2 collective-permute-start.4
  49.7 15.5 %all_to_all.30 = f32[8,8,768]{2,1,0:T(8,128)S(1)} all-to-all(f32[8,8,768]{2,1,0:T(8,128)S(1)} %broadcast_in_dim.21), channel_id=1, replica_groups=mesh['prow'=8,'pcol_0'=4,'pcol_1'=8] {'pcol_1'}, dimensions={0} | all-to-all | bytes 393216 | tf_op jit(solution)/shard_map/all_to_all | solution.py:189
  65.3 0.5 collective-permute-start.7
  65.9 1.1 collective-permute-start.6
  67.0 0.9 broadcast_in_dim.22
  68.0 3.5 %all-to-all-start.4 = ((f32[4,64,768]{2,1,0:T(8,128)}), f32[4,64,768]{2,1,0:T(8,128)S(1)}, u32[]{:S(2)}, u32[]{:S(2)}) async-start(f32[4,64,768]{2,1,0:T(8,128)} %broadcast_in_dim.22), calls=%async_computation.4 | async-start | bytes 1572864 | tf_op jit(solution)/shard_map/all_to_all | solution.py:189
  71.5 4.3 %collective-permute-done.7 = f32[4,64,512]{2,1,0:T(8,128)S(1)} collective-permute-done((f32[4,64,512]{2,1,0:T(8,128)S(1)}, f32[4,64,512]{2,1,0:T(8,128)S(1)}, u32[]{:S(2)}, u32[]{:S(2)}) %collective-permute-start.7) | collective-permute-done | bytes 524320 | tf_op jit(solution)/shard_map/ppermute | solution.py:155
  75.8 1.5 %collective-permute-done.6 = f32[4,64,512]{2,1,0:T(8,128)} collective-permute-done((f32[4,64,512]{2,1,0:T(8,128)S(1)}, f32[4,64,512]{2,1,0:T(8,128)}, u32[]{:S(2)}, u32[]{:S(2)}) %collective-permute-start.6) | collective-permute-done | bytes 524320 | tf_op jit(solution)/shard_map/ppermute | solution.py:155
  77.3 1.2 %add_add_fusion = f32[4,64,512]{2,1,0:T(8,128)S(1)} fusion(f32[4,64,512]{2,1,0:T(8,128)S(1)} %collective-permute-done.7, f32[4,64,512]{2,1,0:T(8,128)S(1)} %copy-done.5, f32[4,64,512]{2,1,0:T(8,128)} %collective-permute-done.6), kind=kLoop, calls=%fused_computation.7 | loop fusion | flops 262144 | bytes 2097152 | tf_op jit(solution)/shard_map/add | solution.py:181
  78.9 2.4 %collective-permute-start.9 = (f32[64,512]{1,0:T(8,128)S(1)}, f32[64,512]{1,0:T(8,128)S(1)}, u32[]{:S(2)}, u32[]{:S(2)}) collective-permute-start(f32[64,512]{1,0:T(8,128)S(1)} %get-tuple-element.51), channel_id=1, source_target_pairs={{0,24},{8,0},{16,8},{24,16},{1,25},{9,1},{17,9},{25,17},{2,26},{10... | collective-permute-start | bytes 393224 | tf_op jit(solution)/shard_map/ppermute | solution.py:155
  81.3 4.3 %collective-permute-done.8 = f32[64,512]{1,0:T(8,128)S(1)} collective-permute-done((f32[64,512]{1,0:T(8,128)S(1)}, f32[64,512]{1,0:T(8,128)S(1)}, u32[]{:S(2)}, u32[]{:S(2)}) %collective-permute-start.8) | collective-permute-done | bytes 131104 | tf_op jit(solution)/shard_map/ppermute | solution.py:155
  85.9 4.8 %collective-permute-done.10 = f32[64,512]{1,0:T(8,128)S(1)} collective-permute-done((f32[64,512]{1,0:T(8,128)S(1)}, f32[64,512]{1,0:T(8,128)S(1)}, u32[]{:S(2)}, u32[]{:S(2)}) %collective-permute-start.10) | collective-permute-done | bytes 131104 | tf_op jit(solution)/shard_map/ppermute | solution.py:155
  90.8 1.6 %offer.1 = f32[8,64,512]{2,1,0:T(8,128)} custom-call(f32[64,512]{1,0:T(8,128)S(1)} %fusion.11.matrix_ref, f32[256,512]{1,0:T(8,128)S(1)} %compare_convert_fusion.pick_ref), custom_call_target="tpu_custom_call" | custom-call | tf_op jit(solution)/shard_map/slab_swap/offer/pallas_call | solution.py:288
  92.4 8.2 %all-to-all-start.5 = ((f32[8,64,512]{2,1,0:T(8,128)}), f32[8,64,512]{2,1,0:T(8,128)S(1)}, u32[]{:S(2)}, u32[]{:S(2)}) async-start(f32[8,64,512]{2,1,0:T(8,128)} %offer.1), calls=%async_computation.5 | async-start | bytes 2097152 | tf_op jit(solution)/shard_map/slab_swap/all_to_all | solution.py:189
  100.8 15.4 %factor.1 = (f32[256,256]{1,0:T(8,128)S(1)}, f32[256,256]{1,0:T(8,128)S(1)}, f32[256,256]{1,0:T(8,128)S(1)}) custom-call(f32[256,256]{1,0:T(8,128)S(1)} %slice.60.t_ref), custom_call_target="tpu_custom_call" | custom-call | flops 40000000 | bytes 60000000 | tf_op jit(solution)/shard_map/factor/pallas_call | solution.py:267
  116.3 2.1 %finish.1 = f32[64,512]{1,0:T(8,128)} custom-call(s32[256,1]{1,0:T(8,128)S(1)} %copy.8.pivot_ref, f32[64,512]{1,0:T(8,128)S(1)} %fusion.11.matrix_ref, f32[8,64,512]{2,1,0:T(8,128)S(1)} %all-to-all-done.5.offers_ref, f32[256,512]{1,0:T(8,128)S(1)} %slice.59.panel_ref, f32[256,256]{1,0:T(8,128)S(1)} %get-tuple-element.48.packed_ref, ...), custom_call_target="tpu_custom_call" | custom-call | tf_op jit(solution)/shard_map/finish/pallas_call | solution.py:327
  (49 shorter events, 1.9 us)
Async XLA Ops:
  2.8 14.7 %copy-start.6 = (s32[1,256]{1,0:T(1,128)S(1)}, s32[1,256]{1,0:T(1,128)}, u32[]{:S(2)}) copy-start(s32[1,256]{1,0:T(1,128)} %param.11) | copy-start | bytes 3076
  2.8 14.8 %all-to-all-start = ((f32[4,64,512]{2,1,0:T(8,128)}), f32[4,64,512]{2,1,0:T(8,128)S(1)}, u32[]{:S(2)}, u32[]{:S(2)}) async-start(f32[4,64,512]{2,1,0:T(8,128)} %panel_blocks.1), calls=%async_computation | async-start | bytes 1048576 | tf_op jit(solution)/shard_map/all_to_all | solution.py:189
  11.8 13.1 %collective-permute-start = (f32[2,64,512]{2,1,0:T(8,128)}, f32[2,64,512]{2,1,0:T(8,128)S(1)}, u32[]{:S(2)}, u32[]{:S(2)}) collective-permute-start(f32[2,64,512]{2,1,0:T(8,128)} %get-tuple-element.32), channel_id=1, source_target_pairs={{0,1},{1,2},{2,3},{3,4},{4,5},{5,6},{6,7},{7,0},{8,9},{9,10},{10,1... | collective-permute-start | bytes 786440 | tf_op jit(solution)/shard_map/ppermute | solution.py:155
  13.4 11.4 %collective-permute-start.1 = (f32[2,64,512]{2,1,0:T(8,128)}, f32[2,64,512]{2,1,0:T(8,128)S(1)}, u32[]{:S(2)}, u32[]{:S(2)}) collective-permute-start(f32[2,64,512]{2,1,0:T(8,128)} %get-tuple-element.33), channel_id=1, source_target_pairs={{0,7},{1,0},{2,1},{3,2},{4,3},{5,4},{6,5},{7,6},{8,15},{9,8},{10,9... | collective-permute-start | bytes 786440 | tf_op jit(solution)/shard_map/ppermute | solution.py:155
  18.3 14.5 %all-to-all-start.1 = ((f32[8,8,512]{2,1,0:T(8,128)}), f32[8,8,512]{2,1,0:T(8,128)S(1)}, u32[]{:S(2)}, u32[]{:S(2)}) async-start(f32[8,8,512]{2,1,0:T(8,128)} %bitcast.2), calls=%async_computation.1 | async-start | bytes 262144 | tf_op jit(solution)/shard_map/all_to_all | solution.py:189
  26.2 21.6 %copy-start.3 = (f32[4,64,512]{2,1,0:T(8,128)S(1)}, f32[4,64,512]{2,1,0:T(8,128)}, u32[]{:S(2)}) copy-start(f32[4,64,512]{2,1,0:T(8,128)} %get-tuple-element.38) | copy-start | bytes 1572868
  26.2 22.2 %copy-start.2 = (f32[4,64,512]{2,1,0:T(8,128)S(1)}, f32[4,64,512]{2,1,0:T(8,128)}, u32[]{:S(2)}) copy-start(f32[4,64,512]{2,1,0:T(8,128)} %get-tuple-element.30) | copy-start | bytes 1572868
  26.3 21.6 %collective-permute-start.3 = (f32[4,64,512]{2,1,0:T(8,128)S(1)}, f32[4,64,512]{2,1,0:T(8,128)S(1)}, u32[]{:S(2)}, u32[]{:S(2)}) collective-permute-start(f32[4,64,512]{2,1,0:T(8,128)S(1)} %pad_maximum_fusion.1), channel_id=1, source_target_pairs={{0,7},{1,0},{2,1},{3,2},{4,3},{5,4},{6,5},{7,6},{8,15},{9,8},{10,9... | collective-permute-start | bytes 1572872 | tf_op jit(solution)/shard_map/ppermute | solution.py:155
  29.8 18.0 %collective-permute-start.2 = (f32[4,64,512]{2,1,0:T(8,128)}, f32[4,64,512]{2,1,0:T(8,128)S(1)}, u32[]{:S(2)}, u32[]{:S(2)}) collective-permute-start(f32[4,64,512]{2,1,0:T(8,128)} %pad_maximum_fusion), channel_id=1, source_target_pairs={{0,1},{1,2},{2,3},{3,4},{4,5},{5,6},{6,7},{7,0},{8,9},{9,10},{10,1... | collective-permute-start | bytes 1572872 | tf_op jit(solution)/shard_map/ppermute | solution.py:155
  34.0 31.3 %copy-start.1 = (f32[4,64,512]{2,1,0:T(8,128)S(1)}, f32[4,64,512]{2,1,0:T(8,128)}, u32[]{:S(2)}) copy-start(f32[4,64,512]{2,1,0:T(8,128)} %get-tuple-element.41) | copy-start | bytes 1572868
  34.0 13.5 %all-to-all-start.2 = ((f32[8,8,512]{2,1,0:T(8,128)}), f32[8,8,512]{2,1,0:T(8,128)S(1)}, u32[]{:S(2)}, u32[]{:S(2)}) async-start(f32[8,8,512]{2,1,0:T(8,128)} %broadcast_in_dim.19), calls=%async_computation.2 | async-start | bytes 262144 | tf_op jit(solution)/shard_map/all_to_all | solution.py:189
  47.9 17.9 %copy-start = (f32[4,64,512]{2,1,0:T(8,128)S(1)}, f32[4,64,512]{2,1,0:T(8,128)}, u32[]{:S(2)}) copy-start(f32[4,64,512]{2,1,0:T(8,128)} %get-tuple-element.29) | copy-start | bytes 1572868
  48.0 17.3 %collective-permute-start.5 = (f32[4,64,512]{2,1,0:T(8,128)S(1)}, f32[4,64,512]{2,1,0:T(8,128)S(1)}, u32[]{:S(2)}, u32[]{:S(2)}) collective-permute-start(f32[4,64,512]{2,1,0:T(8,128)S(1)} %add.52), channel_id=1, source_target_pairs={{0,7},{1,0},{2,1},{3,2},{4,3},{5,4},{6,5},{7,6},{8,15},{9,8},{10,9... | collective-permute-start | bytes 1572872 | tf_op jit(solution)/shard_map/ppermute | solution.py:155
  48.5 16.7 %collective-permute-start.4 = (f32[4,64,512]{2,1,0:T(8,128)S(1)}, f32[4,64,512]{2,1,0:T(8,128)S(1)}, u32[]{:S(2)}, u32[]{:S(2)}) collective-permute-start(f32[4,64,512]{2,1,0:T(8,128)S(1)} %add.51), channel_id=1, source_target_pairs={{0,1},{1,2},{2,3},{3,4},{4,5},{5,6},{6,7},{7,0},{8,9},{9,10},{10,1... | collective-permute-start | bytes 1572872 | tf_op jit(solution)/shard_map/ppermute | solution.py:155
  65.3 12.0 %copy-start.5 = (f32[4,64,512]{2,1,0:T(8,128)S(1)}, f32[4,64,512]{2,1,0:T(8,128)}, u32[]{:S(2)}) copy-start(f32[4,64,512]{2,1,0:T(8,128)} %get-tuple-element.28) | copy-start | bytes 1572868
  65.3 10.5 %collective-permute-start.7 = (f32[4,64,512]{2,1,0:T(8,128)S(1)}, f32[4,64,512]{2,1,0:T(8,128)S(1)}, u32[]{:S(2)}, u32[]{:S(2)}) collective-permute-start(f32[4,64,512]{2,1,0:T(8,128)S(1)} %add.54), channel_id=1, source_target_pairs={{0,7},{1,0},{2,1},{3,2},{4,3},{5,4},{6,5},{7,6},{8,15},{9,8},{10,9... | collective-permute-start | bytes 1572872 | tf_op jit(solution)/shard_map/ppermute | solution.py:155
  65.9 11.3 %collective-permute-start.6 = (f32[4,64,512]{2,1,0:T(8,128)S(1)}, f32[4,64,512]{2,1,0:T(8,128)}, u32[]{:S(2)}, u32[]{:S(2)}) collective-permute-start(f32[4,64,512]{2,1,0:T(8,128)S(1)} %add.53), channel_id=1, source_target_pairs={{0,1},{1,2},{2,3},{3,4},{4,5},{5,6},{6,7},{7,0},{8,9},{9,10},{10,1... | collective-permute-start | bytes 1572872 | tf_op jit(solution)/shard_map/ppermute | solution.py:155
  68.0 13.3 %all-to-all-start.4 = ((f32[4,64,768]{2,1,0:T(8,128)}), f32[4,64,768]{2,1,0:T(8,128)S(1)}, u32[]{:S(2)}, u32[]{:S(2)}) async-start(f32[4,64,768]{2,1,0:T(8,128)} %broadcast_in_dim.22), calls=%async_computation.4 | async-start | bytes 1572864 | tf_op jit(solution)/shard_map/all_to_all | solution.py:189
  71.5 19.2 %copy-start.4 = (f32[64,512]{1,0:T(8,128)S(1)}, f32[64,512]{1,0:T(8,128)}, u32[]{:S(2)}) copy-start(f32[64,512]{1,0:T(8,128)} %slab_ref.1) | copy-start | bytes 393220
  78.5 7.1 %collective-permute-start.8 = (f32[64,512]{1,0:T(8,128)S(1)}, f32[64,512]{1,0:T(8,128)S(1)}, u32[]{:S(2)}, u32[]{:S(2)}) collective-permute-start(f32[64,512]{1,0:T(8,128)S(1)} %get-tuple-element.52), channel_id=1, source_target_pairs={{0,8},{8,16},{16,24},{24,0},{1,9},{9,17},{17,25},{25,1},{2,10},{10... | collective-permute-start | bytes 393224 | tf_op jit(solution)/shard_map/ppermute | solution.py:155
  78.9 6.7 %collective-permute-start.9 = (f32[64,512]{1,0:T(8,128)S(1)}, f32[64,512]{1,0:T(8,128)S(1)}, u32[]{:S(2)}, u32[]{:S(2)}) collective-permute-start(f32[64,512]{1,0:T(8,128)S(1)} %get-tuple-element.51), channel_id=1, source_target_pairs={{0,24},{8,0},{16,8},{24,16},{1,25},{9,1},{17,9},{25,17},{2,26},{10... | collective-permute-start | bytes 393224 | tf_op jit(solution)/shard_map/ppermute | solution.py:155
  85.6 5.1 %collective-permute-start.10 = (f32[64,512]{1,0:T(8,128)S(1)}, f32[64,512]{1,0:T(8,128)S(1)}, u32[]{:S(2)}, u32[]{:S(2)}) collective-permute-start(f32[64,512]{1,0:T(8,128)S(1)} %fusion.8), channel_id=1, source_target_pairs={{0,8},{8,16},{16,24},{24,0},{1,9},{9,17},{17,25},{25,1},{2,10},{10... | collective-permute-start | bytes 393224 | tf_op jit(solution)/shard_map/ppermute | solution.py:155
  92.4 23.8 %all-to-all-start.5 = ((f32[8,64,512]{2,1,0:T(8,128)}), f32[8,64,512]{2,1,0:T(8,128)S(1)}, u32[]{:S(2)}, u32[]{:S(2)}) async-start(f32[8,64,512]{2,1,0:T(8,128)} %offer.1), calls=%async_computation.5 | async-start | bytes 2097152 | tf_op jit(solution)/shard_map/slab_swap/all_to_all | solution.py:189
